TPU v7x, 256 devices: a whole 4x4x8 slice. The times are simulated.
256 devices in a mesh: section: 32 (over z, x), tensor: 8 (over y, core).
Axes of the slice: x: 4, y: 4, z: 8, core: 2. Of those that a mesh axis runs over, the one named last changes fastest.
Arguments:
- grad_in: bfloat16 [24576, 4096], P('section', 'tensor'), may hold values from -6 to 6
- layer_in: bfloat16 [24576, 4096], P('section', 'tensor'), may hold values from -6 to 6
- norm_gain: float32 [32, 4096], P('section', 'tensor'), may hold values from 0.5 to 1.5
- attn_weights: bfloat16 [32, 6, 32, 128, 128], P('section', None, 'tensor'), may hold values from 0 to 2, as said below
- attn_out: bfloat16 [24576, 4096], P('section', 'tensor'), may hold values from -6 to 6
- w_value: bfloat16 [131072, 1024], P(('section', 'tensor')), may hold values from -0.1875 to 0.1875
- w_out: bfloat16 [131072, 4096], P(('section', 'tensor')), may hold values from -0.09375 to 0.09375
- fac_out_in: bfloat16 [32, 32, 4096], P('section', None, 'tensor'), may hold values from -0.09375 to 0.09375
- fac_out_out: bfloat16 [32, 32, 4096], P('section', None, 'tensor'), may hold values from -0.09375 to 0.09375
- fac_val_in: bfloat16 [32, 32, 4096], P('section', None, 'tensor'), may hold values from -0.09375 to 0.09375
- fac_val_out: bfloat16 [32, 32, 1024], P('section', None, 'tensor'), may hold values from -0.1875 to 0.1875
- coef: float32 [32, 2, 16, 32, 32], P('section'), may hold values from -0.3125 to 0.3125
- eig: float32 [32, 2, 32, 32], P('section'), may hold values from 0.01 to 90, as said below
Outputs:
- grad_next: bfloat16 [24576, 4096], P('section', 'tensor')
- scores: float32 [24576, 16], P('section')
Inputs may be any that keep to these rules, and one draw needn't show every extreme that they name: `attn_weights`: zero where the key comes after the query. `eig`: positive.
All inputs are finite; a program needn't handle non-finite values.
Results may differ from a plain program's by a relative error of at most 0.004.
Values may be sent and summed in bfloat16 or wider, within the bound.
A program may use at most 64 MiB of HBM per device.

v0:
```python
import jax
import jax.numpy as jnp
from jax import lax
from jax.sharding import PartitionSpec as P

D = 4096
H = 32
KV = 8
HD = 128
E = 32


def shifted(value, axis, steps):
    count = lax.axis_size(axis)
    leading, last = (max(0, -steps), min(count, count - steps))
    return lax.ppermute(value, axis, [(source, source + steps) for source in range(leading, last)])


def contract(left, right):
    return lax.dot_general(
        left, right, (((1,), (1,)), ((), ())), preferred_element_type=jnp.float32
    )


def per_device(
    grad_in,
    layer_in,
    norm_gain,
    attn_weights,
    attn_out,
    w_value,
    w_out,
    fac_out_in,
    fac_out_out,
    fac_val_in,
    fac_val_out,
    coef,
    eig,
):
    tokens = grad_in.shape[0]
    heads_here = attn_weights.shape[2]
    group = H // KV
    kv_here = heads_here // group
    seqs = attn_weights.shape[1]
    span = attn_weights.shape[3]
    full_grad = lax.all_gather(grad_in, "tensor", axis=1, tiled=True)
    d_att = contract(full_grad, w_out).astype(jnp.bfloat16)
    d_att5 = d_att.reshape(seqs, span, kv_here, group, HD)
    probs5 = attn_weights[0].reshape(seqs, kv_here, group, span, span)
    d_val = jnp.einsum("bkgij,bikge->bjke", probs5, d_att5, preferred_element_type=jnp.float32)
    d_val = d_val.reshape(tokens, kv_here * HD).astype(jnp.bfloat16)
    all_vals = lax.all_gather(d_val, "tensor", axis=1, tiled=True)
    xf = layer_in.astype(jnp.float32)
    gain = norm_gain[0]
    scaled = (xf * gain).astype(jnp.bfloat16)
    sq_local = jnp.sum(xf * xf, axis=-1)
    p_out = contract(attn_out, fac_out_in[0])
    s_out = contract(grad_in, fac_out_out[0])
    p_raw = contract(scaled, fac_val_in[0])
    s_val = contract(d_val, fac_val_out[0])
    stacked = jnp.concatenate([p_out, s_out, p_raw, s_val], axis=1)
    sq_sum = lax.psum(sq_local, "tensor")
    stacked = lax.psum(stacked, "tensor")
    d_norm = contract(all_vals, w_value)
    cross_sum = lax.psum(jnp.sum(xf * gain * d_norm, axis=-1), "tensor")
    inv = lax.rsqrt(sq_sum / D + 1e-05)
    cross = cross_sum / D
    d_x = (
        grad_in.astype(jnp.float32) + inv[:, None] * gain * d_norm - xf * (inv**3 * cross)[:, None]
    )
    grad_next = shifted(d_x.astype(jnp.bfloat16), "section", -1)
    sections = lax.axis_size("section")
    damp = 0.1 * lax.psum(jnp.mean(eig[0]), "section") / sections
    kern = coef[0] / (eig[0][:, None] + damp)
    width = E
    p_out = stacked[:, 0:width]
    s_out = stacked[:, width : 2 * width]
    p_val = inv[:, None] * stacked[:, 2 * width : 3 * width]
    s_val = stacked[:, 3 * width : 4 * width]
    exact = lax.Precision.HIGHEST
    left_o = jnp.einsum("ti,qij->tqj", p_out, kern[0], precision=exact)
    left_v = jnp.einsum("ti,qij->tqj", p_val, kern[1], precision=exact)
    scores = jnp.einsum("tqj,tj->tq", left_o, s_out, precision=exact) + jnp.einsum(
        "tqj,tj->tq", left_v, s_val, precision=exact
    )
    return (grad_next, scores)


def solution(mesh):
    placed = (
        P("section", "tensor"),
        P("section", "tensor"),
        P("section", "tensor"),
        P("section", None, "tensor", None, None),
        P("section", "tensor"),
        P(("section", "tensor"), None),
        P(("section", "tensor"), None),
        P("section", None, "tensor"),
        P("section", None, "tensor"),
        P("section", None, "tensor"),
        P("section", None, "tensor"),
        P("section", None, None, None, None),
        P("section", None, None, None),
    )
    return jax.shard_map(
        per_device,
        mesh=mesh,
        in_specs=placed,
        out_specs=(P("section", "tensor"), P("section", None)),
        check_vma=False,
    )
```

profile of v0, /device:TPU:102, one launch (start us, length us, event | category | flops | bytes accessed | tf_op | source)
XLA Modules:
  0.0 246.7 jit_solution(5617076253678427619)
XLA Ops:
  7.2 0.7 all-gather.3.cloned.1.call-update
  8.0 47.2 %all-gather.3.cloned.1.call-done = bf16[768,4096]{1,0:T(8,128)(2,1)} async-done(((bf16[768,512]{1,0:T(8,128)(2,1)}), bf16[768,4096]{1,0:T(8,128)(2,1)}) %all-gather.3.cloned.1.call-update) | async-done | bytes 6291472 | tf_op jit(solution)/shard_map/all_gather | solution.py:46
  55.2 7.4 %convolution_convert_fusion = bf16[768,512]{1,0:T(8,128)(2,1)S(1)} fusion(bf16[768,4096]{1,0:T(8,128)(2,1)} %all-gather.3.cloned.1.call-done, bf16[512,4096]{1,0:T(8,128)(2,1)} %param.19), kind=kOutput, calls=%fused_computation.11 | convolution fusion | flops 3221618688 | bytes 11272192 | tf_op jit(solution)/shard_map/dot_general | solution.py:20
  62.7 0.2 reshape.30
  62.8 2.3 fusion.6
  65.2 0.6 reduce_sum.29
  66.5 69.9 %psum.31 = f32[]{:T(128)} all-reduce(f32[]{:T(128)S(6)} %div.22), channel_id=1, replica_groups=mesh['section'=32,'tensor'=8] {'section'}, use_global_device_ids=true, to_apply=%region_6.0 | all-reduce | flops 1 | bytes 8 | tf_op jit(solution)/shard_map/psum | solution.py:73
  136.3 0.3 copy.25
  137.4 1.0 copy.29
  138.4 1.4 copy.26
  139.8 1.1 fusion.17
  140.9 2.1 fusion.19
  143.1 1.0 fusion.7
  144.2 3.6 %fusion.3 = (f32[768]{0:T(1024)S(1)}, f32[768]{0:T(1024)S(1)}, f32[768,512]{0,1:T(8,128)}) fusion(bf16[768,512]{0,1:T(8,128)(2,1)S(1)} %copy.26, f32[512]{0:T(512)S(1)} %bitcast.62, bf16[768,1024]{1,0:T(8,128)(2,1)} %all-gather.5.cloned.1.call-done, bf16[512,1024]{1,0:T(8,128)(2,1)S(1)} %copy-done), kind=kOutput, calls=%fused_computation.6 | convolution fusion | flops 807664128 | bytes 4988928 | tf_op jit(solution)/shard_map/dot_general | solution.py:20
  147.8 12.6 %all-reduce = (f32[768]{0:T(1024)S(1)}, f32[768]{0:T(1024)S(1)}) all-reduce(f32[768]{0:T(1024)S(1)} %get-tuple-element.9, f32[768]{0:T(1024)S(1)} %get-tuple-element.8), channel_id=1, replica_groups=mesh['section'=32,'tensor'=8] {'tensor'}, use_global_device_ids=true, to_apply=%region_3.0 | all-reduce | flops 1536 | bytes 12288 | tf_op jit(solution)/shard_map/psum | solution.py:65
  160.5 2.8 %fusion.5 = bf16[768,512]{0,1:T(8,128)(2,1)} fusion(bf16[768,512]{0,1:T(8,128)(2,1)S(1)} %copy.26, f32[768,512]{0,1:T(8,128)} %get-tuple-element.18, bf16[768,512]{0,1:T(8,128)(2,1)S(1)} %copy.25, f32[768]{0:T(1024)S(1)} %get-tuple-element.17, f32[512]{0:T(512)S(1)} %bitcast.63, f32[768]{0:T(1024)S(1)} %get-tuple-element.16), kind=kLoop, calls=%fused_computation.8 | loop fusion | flops 3145728 | bytes 3940352 | tf_op jit(solution)/shard_map/convert_element_type | solution.py:71
  163.3 1.9 collective-permute-start
  165.4 0.8 pad_maximum_fusion
  166.3 66.4 %all-reduce.3.cloned.1.call-done = f32[768,128]{0,1:T(8,128)} async-done(((f32[768,128]{0,1:T(8,128)}), f32[768,128]{0,1:T(8,128)}) %all-reduce.3.cloned.1.call-update) | async-done | bytes 393232 | tf_op jit(solution)/shard_map/psum | solution.py:63
  232.7 1.0 fusion.25
  233.6 2.4 multiply_reduce_fusion.1
  236.0 2.4 multiply_reduce_fusion
  238.3 0.6 add.40
  239.0 1.2 copy.31
  (35 shorter events, 0.6 us)
Async XLA Ops:
  7.2 137.0 %copy-start = (bf16[512,1024]{1,0:T(8,128)(2,1)S(1)}, bf16[512,1024]{1,0:T(8,128)(2,1)}, u32[]{:S(2)}) copy-start(bf16[512,1024]{1,0:T(8,128)(2,1)} %param.18) | copy-start | bytes 3145732
  7.2 48.0 %all-gather.3.cloned.1.call-start = ((), (), s32[]{:S(2)}) async-start(), calls=%async_computation | async-start | bytes 7077888 | tf_op jit(solution)/shard_map/all_gather | solution.py:46
  7.9 136.3 %all-gather.5.cloned.1.call-start = ((), (), s32[]{:S(2)}) async-start(), calls=%async_computation.1 | async-start | bytes 1769472 | tf_op jit(solution)/shard_map/all_gather | solution.py:52
  62.6 2.6 %copy-start.7 = (f32[1,2,32,32]{3,2,1,0:T(8,128)S(1)}, f32[1,2,32,32]{3,2,1,0:T(8,128)}, u32[]{:S(2)}) copy-start(f32[1,2,32,32]{3,2,1,0:T(8,128)} %param.25) | copy-start | bytes 24580
  62.6 73.7 %copy-start.1 = (bf16[768,512]{1,0:T(8,128)(2,1)S(1)}, bf16[768,512]{1,0:T(8,128)(2,1)}, u32[]{:S(2)}) copy-start(bf16[768,512]{1,0:T(8,128)(2,1)} %param.13) | copy-start | bytes 2359300
  65.1 72.2 %copy-start.4 = (f32[1,2,16,32,32]{4,3,2,1,0:T(8,128)S(1)}, f32[1,2,16,32,32]{4,3,2,1,0:T(8,128)}, u32[]{:S(2)}) copy-start(f32[1,2,16,32,32]{4,3,2,1,0:T(8,128)} %param.24) | copy-start | bytes 393220
  65.1 167.5 %all-reduce.3.cloned.1.call-start = ((), (), s32[]{:S(2)}) async-start(), calls=%async_computation.2 | async-start | bytes 786432 | tf_op jit(solution)/shard_map/psum | solution.py:63
  138.4 4.7 %copy-start.9 = (f32[1,512]{1,0:T(1,128)S(1)}, f32[1,512]{1,0:T(1,128)}, u32[]{:S(2)}) copy-start(f32[1,512]{1,0:T(1,128)} %param.15) | copy-start | bytes 6148
  139.8 3.3 %copy-start.8 = (bf16[1,32,512]{2,1,0:T(8,128)(2,1)S(1)}, bf16[1,32,512]{2,1,0:T(8,128)(2,1)}, u32[]{:S(2)}) copy-start(bf16[1,32,512]{2,1,0:T(8,128)(2,1)} %param.22) | copy-start | bytes 98308
  139.8 4.3 %copy-start.2 = (f32[1,2,16,32,32]{3,4,2,1,0:T(8,128)S(1)}, f32[1,2,16,32,32]{3,4,2,1,0:T(8,128)}, u32[]{:S(2)}) copy-start(f32[1,2,16,32,32]{3,4,2,1,0:T(8,128)} %copy.29) | copy-start | bytes 393220
  160.5 4.7 %copy-start.3 = (bf16[6,128,128]{1,2,0:T(8,128)(2,1)S(1)}, bf16[6,128,128]{1,2,0:T(8,128)(2,1)}, u32[]{:S(2)}) copy-start(bf16[6,128,128]{1,2,0:T(8,128)(2,1)} %fusion.6) | copy-start | bytes 589828
  160.5 4.7 %copy-start.10 = (bf16[1,32,128]{2,1,0:T(8,128)(2,1)S(1)}, bf16[1,32,128]{2,1,0:T(8,128)(2,1)}, u32[]{:S(2)}) copy-start(bf16[1,32,128]{2,1,0:T(8,128)(2,1)} %param.23) | copy-start | bytes 24580
  160.5 4.9 %copy-start.5 = (f32[768,32]{0,1:T(8,128)S(1)}, f32[768,32]{0,1:T(8,128)}, u32[]{:S(2)}) copy-start(f32[768,32]{0,1:T(8,128)} %fusion.19) | copy-start | bytes 294916
  160.5 4.9 %copy-start.6 = (f32[768,32]{0,1:T(8,128)S(1)}, f32[768,32]{0,1:T(8,128)}, u32[]{:S(2)}) copy-start(f32[768,32]{0,1:T(8,128)} %fusion.7) | copy-start | bytes 294916
  163.3 75.7 %collective-permute-start = (bf16[768,512]{0,1:T(8,128)(2,1)}, bf16[768,512]{0,1:T(8,128)(2,1)S(1)}, u32[]{:S(2)}, u32[]{:S(2)}) collective-permute-start(bf16[768,512]{0,1:T(8,128)(2,1)} %fusion.5), channel_id=1, source_target_pairs={{8,0},{16,8},{24,16},{32,24},{40,32},{48,40},{56,48},{64,56},{72,6... | collective-permute-start | bytes 2359304 | tf_op jit(solution)/shard_map/ppermute | solution.py:16
Sparse Core Ops, SparseCore 0:
  9.9 45.2 all-gather.2
  65.3 27.8 all-gather.4
  166.4 66.2 all-reduce.2
where the time goes:
time: 248 us; the launch traced here: 247 us
  waiting for transfers between devices  114 us (46%)
  blocking collectives  82.5 us (33%)
  matrix products  22.5 us (9%)
  between operations  15.3 us (6%)
  local copies, waits for them, and re-layouts  5.15 us (2%)
  other arithmetic  4.9 us (2%)
    psum x1, blocking collectives, per_device(): damp = 0.1 * lax.psum(jnp.mean(eig[0]), 'section') / sections  69.9 us
    psum x1, waiting for transfers between devices, per_device(): stacked = lax.psum(stacked, 'tensor')  66.4 us
    all_gather x1, waiting for transfers between devices, per_device(): full_grad = lax.all_gather(grad_in, 'tensor', axis=1, tiled=True)  47.2 us
    dot_general x6, matrix products, contract(): lax.dot_general(left, right, (((1,), (1,)), ((), ())), preferred_element_...  15.5 us
    psum x1, blocking collectives, per_device(): cross_sum = lax.psum(jnp.sum(xf * gain * d_norm, axis=-1), 'tensor')  12.6 us
  transfers between devices with their start and end apart: 4, of which 2 were waited for; matrix products, arithmetic and copies ran while one was open for 6% of the time, Pallas kernels for 0%

commit v1 on v0

v1 whole, which is shorter than its diff:
```python
import functools

import jax
import jax.numpy as jnp
from jax import lax
from jax.experimental import pallas as pl
from jax.experimental.pallas import tpu as pltpu
from jax.sharding import PartitionSpec as P

D = 4096
E = 32
Q = 16
SEQS = 6
LEN = 128
W = 512
HD = 128
T = 8
HALF = LEN // 2
MESH = pl.DeviceIdType.MESH
F32 = jnp.float32
BF16 = jnp.bfloat16
HIGH = lax.Precision.HIGHEST


def contract(left, right):
    return lax.dot_general(left, right, (((1,), (1,)), ((), ())), preferred_element_type=F32)


def lanes_folded(value):
    return value[:, 0:128] + value[:, 128:256] + value[:, 256:384] + value[:, 384:512]


def kernel(
    nsec,
    nx,
    dy_h,
    x_h,
    g_h,
    aw_h,
    ao_h,
    wv_h,
    wo_h,
    foi_h,
    foo_h,
    fvi_h,
    fvo_h,
    coef_h,
    eig_h,
    gn_h,
    sc_h,
    dyf,
    dvf,
    x_v,
    ao_v,
    aw_v,
    wv_v,
    wo_v,
    fo_v,
    fs_v,
    fp_v,
    fvof,
    g_v,
    coef_v,
    eig_v,
    du_v,
    dx_v,
    zero_v,
    p_part,
    p_sib,
    p_snd,
    p_rcv,
    sqt,
    rb,
    mb,
    eb1,
    eb2,
    wk,
    sc_v,
    lsem,
    dy_ss,
    dy_rs,
    dv_ss,
    dv_rs,
    m_ss,
    m_rs,
    sq_ss,
    sq_rs,
    fv_ss,
    fv_rs,
    e1_ss,
    e1_rs,
    e2_ss,
    e2_rs,
    ps_ss,
    ps_rs,
    pr_ss,
    pr_rs,
    sc_ss,
    sc_rs,
    dx_ss,
    dx_rs,
):
    nz = nsec // nx
    s = lax.axis_index("section")
    t = lax.axis_index("tensor")
    core = lax.rem(t, 2)
    chip = t // 2
    right = lax.rem(t + 2, T)
    left = lax.rem(t + 6, T)
    across = lax.rem(t + 4, T)
    sib = t + 1 - 2 * core
    sx = lax.rem(s, nx)
    sz = s // nx

    def remote(src, dst, ss, rs, **where):
        return pltpu.make_async_remote_copy(
            src_ref=src, dst_ref=dst, send_sem=ss, recv_sem=rs, device_id=where, device_id_type=MESH
        )

    loads = [
        pltpu.make_async_copy(dy_h, dyf.at[t], lsem.at[0]),
        pltpu.make_async_copy(ao_h, ao_v, lsem.at[1]),
        pltpu.make_async_copy(x_h, x_v, lsem.at[2]),
        pltpu.make_async_copy(g_h, g_v, lsem.at[3]),
        pltpu.make_async_copy(foi_h.at[0], fo_v.at[pl.ds(0, E)], lsem.at[4]),
        pltpu.make_async_copy(foo_h.at[0], fs_v.at[pl.ds(E, E)], lsem.at[5]),
        pltpu.make_async_copy(fvi_h.at[0], fp_v.at[pl.ds(2 * E, E)], lsem.at[6]),
        pltpu.make_async_copy(eig_h.at[0], eig_v, lsem.at[7]),
        pltpu.make_async_copy(wo_h, wo_v, lsem.at[8]),
        pltpu.make_async_copy(aw_h.at[0], aw_v, lsem.at[9]),
        pltpu.make_async_copy(wv_h, wv_v, lsem.at[10]),
        pltpu.make_async_copy(coef_h.at[0], coef_v, lsem.at[11]),
        pltpu.make_async_copy(fvo_h.at[0], fvof.at[t, pl.ds(E, E)], lsem.at[12]),
    ]

    fo_v[...] = jnp.zeros_like(fo_v)
    fs_v[...] = jnp.zeros_like(fs_v)
    fp_v[...] = jnp.zeros_like(fp_v)
    fvof[...] = jnp.zeros_like(fvof)
    wk[...] = jnp.zeros_like(wk)

    barrier = pltpu.get_barrier_semaphore()
    for d in range(1, T):
        pl.semaphore_signal(
            barrier, inc=1, device_id={"tensor": lax.rem(t + d, T)}, device_id_type=MESH
        )
    for d in range(1, nx):
        pl.semaphore_signal(
            barrier, inc=1, device_id={"section": sz * nx + lax.rem(sx + d, nx)}, device_id_type=MESH
        )
    for d in range(1, nz):
        pl.semaphore_signal(
            barrier, inc=1, device_id={"section": lax.rem(sz + d, nz) * nx + sx}, device_id_type=MESH
        )
    pl.semaphore_signal(
        barrier, inc=1, device_id={"section": lax.rem(s + 1, nsec)}, device_id_type=MESH
    )
    for load in loads:
        load.start()
    pl.semaphore_wait(barrier, (T - 1) + (nx - 1) + (nz - 1) + 1)

    def ring_copy(kind, b, buf, own, ss, rs):
        low, high, whole = pl.ds(0, HALF), pl.ds(HALF, HALF), pl.ds(0, LEN)
        source, rows, target = [
            (t, low, right),
            (t, high, right),
            (t, low, left),
            (t, high, left),
            (left, low, right),
            (right, high, left),
            (t, whole, sib),
            (left, whole, sib),
            (right, whole, sib),
            (across, low, sib),
            (across, high, sib),
        ][kind]
        src = buf.at[source, b, rows]
        if own is not None and kind in (0, 1, 2, 3, 6):
            src = own.at[b, rows]
        return remote(
            src, buf.at[source, b, rows], ss.at[kind, b], rs.at[kind, b], tensor=target
        )

    def dy_copy(kind, b):
        return ring_copy(kind, b, dyf, dy_h, dy_ss, dy_rs)

    def dv_copy(kind, b):
        return ring_copy(kind, b, dvf, None, dv_ss, dv_rs)

    def start_own(copy, b):
        for kind in (0, 3, 1, 2, 6):
            copy(kind, b).start()

    def pass_on(copy, b):
        copy(0, b).wait_recv()
        copy(4, b).start()
        copy(3, b).wait_recv()
        copy(5, b).start()

    def pass_sib(copy, b):
        copy(1, b).wait_recv()
        copy(7, b).start()
        copy(2, b).wait_recv()
        copy(8, b).start()

    def pass_across(copy, b):
        copy(4, b).wait_recv()
        copy(9, b).start()
        copy(5, b).wait_recv()
        copy(10, b).start()

    def wait_rest(copy, b):
        for kind in (6, 7, 8, 9, 10):
            copy(kind, b).wait_recv()

    def spread(src, dst, ss, rs, d):
        return remote(src, dst, ss, rs, tensor=lax.rem(t + d, T))

    def m_copy(b, d):
        return spread(mb.at[b, t], mb.at[b, t], m_ss.at[b, d], m_rs.at[b, d], d)

    def sq_copy(d):
        return spread(sqt.at[t], sqt.at[t], sq_ss.at[d], sq_rs.at[d], d)

    def fv_copy(d):
        return spread(
            fvo_h.at[0], fvof.at[t, pl.ds(E, E)], fv_ss.at[d], fv_rs.at[d], d
        )

    def sc_copy(d):
        return spread(
            sc_v, sc_h.at[:, pl.ds(t * 16, 16)], sc_ss.at[d], sc_rs.at[d], d
        )

    def e1_copy(d):
        return remote(
            eb1.at[sx],
            eb1.at[sx],
            e1_ss.at[d],
            e1_rs.at[d],
            section=sz * nx + lax.rem(sx + d, nx),
        )

    def e2_copy(d):
        return remote(
            eb2.at[sz],
            eb2.at[sz],
            e2_ss.at[d],
            e2_rs.at[d],
            section=lax.rem(sz + d, nz) * nx + sx,
        )

    def ps_copy():
        return remote(p_part.at[1 - core], p_sib, ps_ss, ps_rs, tensor=sib)

    def pr_copy(d):
        other = lax.rem(chip + d, 4)
        return remote(
            p_snd.at[other], p_rcv.at[chip], pr_ss.at[d], pr_rs.at[d], tensor=2 * other + core
        )

    def dx_copy(b):
        return remote(
            dx_v.at[b],
            gn_h.at[b],
            dx_ss.at[b],
            dx_rs.at[b],
            section=lax.rem(s + nsec - 1, nsec),
        )

    def zero_copy():
        return pltpu.make_async_copy(zero_v, gn_h, lsem.at[13])

    start_own(dy_copy, 0)
    start_own(dy_copy, 1)
    for d in range(1, T):
        fv_copy(d).start()

    @pl.when(s == nsec - 1)
    def _():
        zero_v[...] = jnp.zeros_like(zero_v)
        zero_copy().start()

    loads[7].wait()
    ev = eig_v[...]
    eb1[sx] = jnp.full((1, 128), jnp.sum(ev[0] + ev[1]), F32)
    for d in range(1, nx):
        e1_copy(d).start()

    for at in (0, 1, 2, 3, 4, 5, 6):
        loads[at].wait()

    def project(b, carry):
        xf = x_v[b].astype(F32)
        scaled = (xf * g_v[...]).astype(BF16)
        sums = jnp.sum(lanes_folded(xf * xf).T, axis=0, keepdims=True)
        sqt[t, b] = sums
        part = contract(ao_v[b], fo_v[...])
        part += contract(dyf[t, b], fs_v[...])
        part += contract(scaled, fp_v[...])
        part = part.reshape(4, 2, 16, 128)
        p_part[0, :, b] = part[:, 0]
        p_part[1, :, b] = part[:, 1]
        return carry

    lax.fori_loop(0, SEQS, project, 0)
    for d in range(1, T):
        sq_copy(d).start()
    ps_copy().start()
    for at in (8, 9, 10, 11, 12):
        loads[at].wait()

    def step(i, carry):
        @pl.when(i < SEQS)
        def _():
            pass_on(dy_copy, i)

        @pl.when(i + 2 < SEQS)
        def _():
            start_own(dy_copy, i + 2)

        @pl.when((i >= 1) & (i < SEQS + 1))
        def _():
            pass_on(dv_copy, i - 1)

        @pl.when(i < SEQS)
        def _():
            pass_sib(dy_copy, i)

        @pl.when((i >= 1) & (i < SEQS + 1))
        def _():
            pass_sib(dv_copy, i - 1)

        @pl.when((i >= 2) & (i < SEQS + 2))
        def _():
            b = i - 2
            wait_rest(dv_copy, b)
            vals = jnp.concatenate([dvf[k, b] for k in range(T)], axis=1)
            du = contract(vals, wv_v[...])
            du_v[b] = du
            cross = x_v[b].astype(F32) * g_v[...] * du
            mb[b, t] = jnp.sum(lanes_folded(cross).T, axis=0, keepdims=True)
            for d in range(1, T):
                m_copy(b, d).start()

        @pl.when(i >= 3)
        def _():
            b = i - 3
            for d in range(1, T):
                m_copy(b, d).wait_recv()
            total = mb[b, 0]
            for k in range(1, T):
                total += mb[b, k]
            mean = jnp.broadcast_to(total * (1.0 / D), (LEN, 128)).T
            inv = rb[b]
            cubed = inv * inv * inv * mean
            for k in range(4):
                cols = slice(k * 128, (k + 1) * 128)
                dx = (
                    dyf[t, b, :, cols].astype(F32)
                    + inv * g_v[:, cols] * du_v[b, :, cols]
                    - x_v[b, :, cols].astype(F32) * cubed
                )
                dx_v[b, :, cols] = dx.astype(BF16)

            @pl.when(s > 0)
            def _():
                dx_copy(b).start()

        @pl.when(i == 0)
        def _():
            ps_copy().wait_recv()
            p_snd[...] = p_part[core] + p_sib[...]
            for d in range(1, 4):
                pr_copy(d).start()
            for d in range(1, nx):
                e1_copy(d).wait_recv()
            eb2[sz] = jnp.sum(eb1[...], axis=0)
            for d in range(1, nz):
                e2_copy(d).start()

        @pl.when(i == 1)
        def _():
            for d in range(1, T):
                sq_copy(d).wait_recv()

            def turn(b, carry):
                total = sqt[0, b]
                for k in range(1, T):
                    total += sqt[k, b]
                inv = lax.rsqrt(total * (1.0 / D) + 1e-05)
                rb[b] = jnp.broadcast_to(inv, (LEN, 128)).T
                return carry

            lax.fori_loop(0, SEQS, turn, 0)

        @pl.when(i == 2)
        def _():
            for d in range(1, nz):
                e2_copy(d).wait_recv()
            damp = jnp.sum(eb2[...], axis=0) * (0.1 / (nsec * 2 * E * E))
            damp = damp[:, 0:E]
            for m in range(2):
                under = eig_v[m] + damp
                for q in range(Q):
                    wk[m * 2 * E : m * 2 * E + E, m * 1024 + q * E : m * 1024 + (q + 1) * E] = (
                        coef_v[m, q] / under
                    )
            row = lax.broadcasted_iota(jnp.int32, (E, W), 0)
            col = lax.broadcasted_iota(jnp.int32, (E, W), 1)
            wk[E : 2 * E, W : 2 * W] = (lax.rem(col, E) == row).astype(F32)

        @pl.when(i < SEQS)
        def _():
            pass_across(dy_copy, i)

        @pl.when((i >= 1) & (i < SEQS + 1))
        def _():
            pass_across(dv_copy, i - 1)

        @pl.when(i < SEQS)
        def _():
            wait_rest(dy_copy, i)
            acc = contract(dyf[0, i], wo_v[:, 0:W])
            for k in range(1, T):
                acc += contract(dyf[k, i], wo_v[:, k * W : (k + 1) * W])
            d_att = acc.astype(BF16)
            d_att = jnp.concatenate([d_att[:, h * HD : (h + 1) * HD] for h in range(4)], axis=0)
            probs = aw_v[i].reshape(4 * LEN, LEN)
            d_val = lax.dot_general(
                probs, d_att, (((0,), (0,)), ((), ())), preferred_element_type=F32
            )
            dvf[t, i] = d_val.astype(BF16)
            start_own(dv_copy, i)

        return carry

    lax.fori_loop(0, SEQS + 3, step, 0)

    for d in range(1, T):
        fv_copy(d).wait_recv()
    for d in range(1, 4):
        pr_copy(d).wait_recv()
    mine = pl.ds(t * 16, 16)
    proj = p_snd[chip]
    for d in range(1, 4):
        proj += p_rcv[lax.rem(chip + d, 4)]
    proj = proj.reshape(96, 128)
    inv = rb[:, mine, :].reshape(96, 128)
    vals = dvf[0, :, mine, :].reshape(96, 128)
    s_val = contract(vals, fvof[0])
    for k in range(1, T):
        s_val += contract(dvf[k, :, mine, :].reshape(96, 128), fvof[k])
    pick = wk[:, W : 2 * W]
    left_o = jnp.dot(proj, wk[:, 0:W], precision=HIGH, preferred_element_type=F32)
    left_v = jnp.dot(proj * inv, wk[:, 2 * W : 3 * W], precision=HIGH, preferred_element_type=F32)
    tiled_o = jnp.dot(proj, pick, precision=HIGH, preferred_element_type=F32)
    tiled_v = jnp.dot(s_val, pick, precision=HIGH, preferred_element_type=F32)
    both = left_o * tiled_o + left_v * tiled_v
    row = lax.broadcasted_iota(jnp.int32, (W, 128), 0)
    col = lax.broadcasted_iota(jnp.int32, (W, 128), 1)
    group = (row // E == col).astype(F32)
    scores = jnp.dot(both, group, precision=HIGH, preferred_element_type=F32)
    sc_v[...] = scores[:, 0:Q].reshape(SEQS, 16, Q)
    keep = pltpu.make_async_copy(sc_v, sc_h.at[:, mine], lsem.at[14])
    keep.start()
    for d in range(1, T):
        sc_copy(d).start()

    def drain(b, carry):
        for kind in range(11):
            dy_copy(kind, b).wait_send()
            dv_copy(kind, b).wait_send()
        for d in range(1, T):
            m_copy(b, d).wait_send()

        @pl.when(s > 0)
        def _():
            dx_copy(b).wait_send()

        @pl.when(s < nsec - 1)
        def _():
            dx_copy(b).wait_recv()

        return carry

    lax.fori_loop(0, SEQS, drain, 0)
    for d in range(1, T):
        sq_copy(d).wait_send()
        fv_copy(d).wait_send()
    for d in range(1, nx):
        e1_copy(d).wait_send()
    for d in range(1, nz):
        e2_copy(d).wait_send()
    ps_copy().wait_send()
    for d in range(1, 4):
        pr_copy(d).wait_send()

    @pl.when(s == nsec - 1)
    def _():
        zero_copy().wait()

    keep.wait()
    for d in range(1, T):
        sc_copy(d).wait()


def per_device(nsec, nx, *arrays):
    (dy, x, g, aw, ao, wv, wo, foi, foo, fvi, fvo, coef, eig) = arrays
    nz = nsec // nx
    blocks = (SEQS, LEN, W)
    dma = pltpu.SemaphoreType.DMA
    vmem = pltpu.VMEM
    anywhere = pl.BlockSpec(memory_space=pl.ANY)
    grad_next, scores = pl.pallas_call(
        functools.partial(kernel, nsec, nx),
        out_shape=(
            jax.ShapeDtypeStruct(blocks, BF16),
            jax.ShapeDtypeStruct((SEQS, LEN, Q), F32),
        ),
        in_specs=[anywhere] * 13,
        out_specs=(anywhere, anywhere),
        scratch_shapes=[
            vmem((T, *blocks), BF16),
            vmem((T, SEQS, LEN, HD), BF16),
            vmem(blocks, BF16),
            vmem(blocks, BF16),
            vmem((SEQS, 4, LEN, LEN), BF16),
            vmem((W, 2 * W), BF16),
            vmem((W, D), BF16),
            vmem((128, W), BF16),
            vmem((128, W), BF16),
            vmem((128, W), BF16),
            vmem((T, 128, HD), BF16),
            vmem((1, W), F32),
            vmem((2, Q, E, E), F32),
            vmem((2, E, E), F32),
            vmem(blocks, F32),
            vmem(blocks, BF16),
            vmem(blocks, BF16),
            vmem((2, 4, SEQS, 16, 128), F32),
            vmem((4, SEQS, 16, 128), F32),
            vmem((4, SEQS, 16, 128), F32),
            vmem((4, SEQS, 16, 128), F32),
            vmem((T, SEQS, 1, 128), F32),
            vmem((SEQS, LEN, 128), F32),
            vmem((SEQS, T, 1, 128), F32),
            vmem((nx, 1, 128), F32),
            vmem((nz, 1, 128), F32),
            vmem((128, 3 * W), F32),
            vmem((SEQS, 16, Q), F32),
            dma((15,)),
            dma((11, SEQS)),
            dma((11, SEQS)),
            dma((11, SEQS)),
            dma((11, SEQS)),
            dma((SEQS, T)),
            dma((SEQS, T)),
            dma((T,)),
            dma((T,)),
            dma((T,)),
            dma((T,)),
            dma((nx,)),
            dma((nx,)),
            dma((nz,)),
            dma((nz,)),
            dma,
            dma,
            dma((4,)),
            dma((4,)),
            dma((T,)),
            dma((T,)),
            dma((SEQS,)),
            dma((SEQS,)),
        ],
        compiler_params=pltpu.CompilerParams(
            collective_id=0, has_side_effects=True, vmem_limit_bytes=48 * 2**20
        ),
        cost_estimate=pl.CostEstimate(
            flops=8 * 10**9, bytes_accessed=10 * 2**20, transcendentals=0
        ),
    )(
        dy.reshape(blocks),
        x.reshape(blocks),
        g,
        aw,
        ao.reshape(blocks),
        wv,
        wo,
        foi,
        foo,
        fvi,
        fvo,
        coef,
        eig,
    )
    return grad_next.reshape(SEQS * LEN, W), scores.reshape(SEQS * LEN, Q)


def solution(mesh):
    nsec = mesh.shape["section"]
    nx = 4 if nsec >= 16 else 2
    placed = (
        P("section", "tensor"),
        P("section", "tensor"),
        P("section", "tensor"),
        P("section", None, "tensor", None, None),
        P("section", "tensor"),
        P(("section", "tensor"), None),
        P(("section", "tensor"), None),
        P("section", None, "tensor"),
        P("section", None, "tensor"),
        P("section", None, "tensor"),
        P("section", None, "tensor"),
        P("section", None, None, None, None),
        P("section", None, None, None),
    )
    return jax.shard_map(
        functools.partial(per_device, nsec, nx),
        mesh=mesh,
        in_specs=placed,
        out_specs=(P("section", "tensor"), P("section", None)),
        check_vma=False,
    )
```

time: 248 us -> 106 us (0.43)
  the two profiles are of different devices: /device:TPU:102 before, /device:TPU:1 now
where the time goes in v1:
time: 106 us; the launch traced here: 105 us
  Pallas kernels  91.7 us (87%)
  local copies, waits for them, and re-layouts  12.8 us (12%)
    pallas_call x1, Pallas kernels, per_device(): pl.pallas_call(functools.partial(kernel, nsec, nx), out_shape=(jax.ShapeD...  91.7 us
    unnamed x26, local copies, waits for them, and re-layouts  12.8 us

profile of v1, /device:TPU:1, one launch (start us, length us, event | category | flops | bytes accessed | tf_op | source)
XLA Modules:
  0.0 105.2 jit_solution(12197837985585862206)
XLA Ops:
  0.6 0.0 copy-start
  0.6 1.2 %copy-done = bf16[512,1024]{1,0:T(8,128)(2,1)S(1)} copy-done((bf16[512,1024]{1,0:T(8,128)(2,1)S(1)}, bf16[512,1024]{1,0:T(8,128)(2,1)}, u32[]{:S(2)}) %copy-start) | copy-done | bytes 1048600
  1.9 0.0 copy-start.1
  1.9 1.1 %copy-done.1 = bf16[768,512]{1,0:T(8,128)(2,1)S(1)} copy-done((bf16[768,512]{1,0:T(8,128)(2,1)S(1)}, bf16[768,512]{1,0:T(8,128)(2,1)}, u32[]{:S(2)}) %copy-start.1) | copy-done | bytes 786456
  3.0 0.0 copy-start.2
  3.0 1.1 %copy-done.2 = bf16[768,512]{1,0:T(8,128)(2,1)S(1)} copy-done((bf16[768,512]{1,0:T(8,128)(2,1)S(1)}, bf16[768,512]{1,0:T(8,128)(2,1)}, u32[]{:S(2)}) %copy-start.2) | copy-done | bytes 786456
  4.1 0.0 copy-start.3
  4.1 1.1 %copy-done.3 = bf16[1,6,4,128,128]{4,3,2,1,0:T(8,128)(2,1)S(1)} copy-done((bf16[1,6,4,128,128]{4,3,2,1,0:T(8,128)(2,1)S(1)}, bf16[1,6,4,128,128]{4,3,2,1,0:T(8,128)(2,1)}, u32[]{:S(2)}) %copy-start.3) | copy-done | bytes 786456
  5.3 0.0 copy-start.4
  5.3 1.1 %copy-done.4 = bf16[768,512]{1,0:T(8,128)(2,1)S(1)} copy-done((bf16[768,512]{1,0:T(8,128)(2,1)S(1)}, bf16[768,512]{1,0:T(8,128)(2,1)}, u32[]{:S(2)}) %copy-start.4) | copy-done | bytes 786456
  6.4 0.0 copy-start.5
  6.4 1.0 copy-done.5
  7.4 0.0 copy-start.6
  7.4 0.8 copy-done.6
  8.2 0.0 copy-start.7
  8.2 0.8 copy-done.7
  9.0 0.0 copy-start.8
  9.0 0.8 copy-done.8
  9.7 0.8 copy-done.9
  10.5 0.7 copy-done.10
  11.2 0.7 copy-done.11
  11.9 91.7 %shard_map.140 = (bf16[6,128,512]{2,1,0:T(8,128)(2,1)S(1)}, f32[6,128,16]{2,1,0:T(8,128)S(1)}) custom-call(bf16[6,128,512]{2,1,0:T(8,128)(2,1)S(1)} %bitcast.7, bf16[6,128,512]{2,1,0:T(8,128)(2,1)S(1)} %bitcast.8, f32[1,512]{1,0:T(1,128)S(1)} %copy-done.11, bf16[1,6,4,128,128]{4,3,2,1,0:T(8,128)(2,1)S(1)} %copy-done.3, bf16[6,128,512]{2,1,0:T(8,128)(2,1)S(1)} %bitcast.9, ...), custom_call_target="tpu_custom_call" | custom-call | flops 8000000000 | bytes 10485760 | tf_op jit(solution)/shard_map/pallas_call | solution.py:515
  103.6 0.8 copy.15
  104.4 0.9 copy.17
  (3 shorter events, 0.0 us)
Async XLA Ops:
  0.6 1.2 %copy-start = (bf16[512,1024]{1,0:T(8,128)(2,1)S(1)}, bf16[512,1024]{1,0:T(8,128)(2,1)}, u32[]{:S(2)}) copy-start(bf16[512,1024]{1,0:T(8,128)(2,1)} %wv_h.1) | copy-start | bytes 3145732
  1.9 1.1 %copy-start.1 = (bf16[768,512]{1,0:T(8,128)(2,1)S(1)}, bf16[768,512]{1,0:T(8,128)(2,1)}, u32[]{:S(2)}) copy-start(bf16[768,512]{1,0:T(8,128)(2,1)} %param.13) | copy-start | bytes 2359300
  3.0 1.1 %copy-start.2 = (bf16[768,512]{1,0:T(8,128)(2,1)S(1)}, bf16[768,512]{1,0:T(8,128)(2,1)}, u32[]{:S(2)}) copy-start(bf16[768,512]{1,0:T(8,128)(2,1)} %param.14) | copy-start | bytes 2359300
  4.1 1.1 %copy-start.3 = (bf16[1,6,4,128,128]{4,3,2,1,0:T(8,128)(2,1)S(1)}, bf16[1,6,4,128,128]{4,3,2,1,0:T(8,128)(2,1)}, u32[]{:S(2)}) copy-start(bf16[1,6,4,128,128]{4,3,2,1,0:T(8,128)(2,1)} %aw_h.1) | copy-start | bytes 2359300
  5.3 1.1 %copy-start.4 = (bf16[768,512]{1,0:T(8,128)(2,1)S(1)}, bf16[768,512]{1,0:T(8,128)(2,1)}, u32[]{:S(2)}) copy-start(bf16[768,512]{1,0:T(8,128)(2,1)} %param.17) | copy-start | bytes 2359300
  6.4 1.0 copy-start.5
  7.4 0.8 copy-start.6
  8.2 0.8 copy-start.7
  9.0 0.8 copy-start.8
  9.7 0.8 copy-start.9
  10.5 0.7 copy-start.10
  11.2 0.7 copy-start.11

commit v2 on v1

v2 whole, which is shorter than its diff:
```python
import functools

import jax
import jax.numpy as jnp
from jax import lax
from jax.experimental import pallas as pl
from jax.experimental.pallas import tpu as pltpu
from jax.sharding import PartitionSpec as P

D = 4096
E = 32
Q = 16
SEQS = 6
LEN = 128
W = 512
HD = 128
T = 8
HALF = LEN // 2
MESH = pl.DeviceIdType.MESH
LIMIT = 64_600_000
F32 = jnp.float32
BF16 = jnp.bfloat16
HIGH = lax.Precision.HIGHEST


def contract(left, right):
    return lax.dot_general(left, right, (((1,), (1,)), ((), ())), preferred_element_type=F32)


def lanes_folded(value):
    return value[:, 0:128] + value[:, 128:256] + value[:, 256:384] + value[:, 384:512]


def kernel(
    nsec,
    dy_h,
    x_h,
    g_h,
    aw_h,
    ao_h,
    wv_h,
    wo_h,
    foi_h,
    foo_h,
    fvi_h,
    fvo_h,
    coef_h,
    eig_h,
    gn_h,
    sc_h,
    dyf,
    dvf,
    x_v,
    ao_v,
    aw_v,
    wv_v,
    wo_v,
    fo_v,
    fs_v,
    fp_v,
    fvof,
    g_v,
    coef_v,
    eig_v,
    du_v,
    dx_v,
    p_part,
    p_sib,
    p_snd,
    p_rcv,
    sqt,
    rb,
    mb,
    ev,
    wk,
    sc_v,
    lsem,
    dy_ss,
    dy_rs,
    dv_ss,
    dv_rs,
    m_ss,
    m_rs,
    e_ss,
    e_rs,
    xs,
):
    phases = nsec.bit_length() - 1
    s = lax.axis_index("section")
    t = lax.axis_index("tensor")
    core = lax.rem(t, 2)
    chip = t // 2
    right = lax.rem(t + 2, T)
    left = lax.rem(t + 6, T)
    across = lax.rem(t + 4, T)
    sib = t + 1 - 2 * core

    def partner(phase):
        bit = lax.rem(s // 2**phase, 2)
        return s + 2**phase * (1 - 2 * bit)

    def remote(src, dst, ss, rs, **where):
        return pltpu.make_async_remote_copy(
            src_ref=src, dst_ref=dst, send_sem=ss, recv_sem=rs, device_id=where, device_id_type=MESH
        )

    loads = [
        pltpu.make_async_copy(dy_h, dyf.at[t], lsem.at[0]),
        pltpu.make_async_copy(ao_h, ao_v, lsem.at[1]),
        pltpu.make_async_copy(x_h, x_v, lsem.at[2]),
        pltpu.make_async_copy(g_h, g_v, lsem.at[3]),
        pltpu.make_async_copy(foi_h.at[0], fo_v.at[pl.ds(0, E)], lsem.at[4]),
        pltpu.make_async_copy(foo_h.at[0], fs_v.at[pl.ds(E, E)], lsem.at[5]),
        pltpu.make_async_copy(fvi_h.at[0], fp_v.at[pl.ds(2 * E, E)], lsem.at[6]),
        pltpu.make_async_copy(eig_h.at[0], eig_v, lsem.at[7]),
        pltpu.make_async_copy(wo_h, wo_v, lsem.at[8]),
        pltpu.make_async_copy(aw_h.at[0], aw_v, lsem.at[9]),
        pltpu.make_async_copy(wv_h, wv_v, lsem.at[10]),
        pltpu.make_async_copy(coef_h.at[0], coef_v, lsem.at[11]),
        pltpu.make_async_copy(fvo_h.at[0], fvof.at[t, pl.ds(E, E)], lsem.at[12]),
    ]

    fo_v[...] = jnp.zeros_like(fo_v)
    fs_v[...] = jnp.zeros_like(fs_v)
    fp_v[...] = jnp.zeros_like(fp_v)
    fvof[...] = jnp.zeros_like(fvof)

    barrier = pltpu.get_barrier_semaphore()
    for d in range(1, T):
        pl.semaphore_signal(
            barrier, inc=1, device_id={"tensor": lax.rem(t + d, T)}, device_id_type=MESH
        )
    for phase in range(phases):
        pl.semaphore_signal(
            barrier, inc=1, device_id={"section": partner(phase)}, device_id_type=MESH
        )
    pl.semaphore_signal(
        barrier, inc=1, device_id={"section": lax.rem(s + 1, nsec)}, device_id_type=MESH
    )
    for load in loads:
        load.start()
    pl.semaphore_wait(barrier, (T - 1) + phases + 1)

    low, high, whole = pl.ds(0, HALF), pl.ds(HALF, HALF), pl.ds(0, LEN)
    routes = [
        (t, low, right, 0),
        (t, high, left, 0),
        (t, high, right, 1),
        (t, low, left, 1),
        (left, low, right, 2),
        (right, high, left, 2),
        (t, whole, sib, 3),
        (left, whole, sib, 3),
        (right, whole, sib, 3),
        (across, low, sib, 3),
        (across, high, sib, 3),
    ]

    class Gather:
        def __init__(self, buf, own, ss, rs):
            self.buf, self.own, self.ss, self.rs = buf, own, ss, rs

        def send(self, b, *kinds):
            for kind in kinds:
                source, rows, target, group = routes[kind]
                dst = self.buf.at[source, b, rows]
                src = dst
                if self.own is not None and kind in (0, 1, 2, 3, 6):
                    src = self.own.at[b, rows]
                remote(src, dst, self.ss.at[b], self.rs.at[group, b], tensor=target).start()

        def arrived(self, b, group):
            blocks = self.buf.at[pl.ds(0, 4 if group == 3 else 1), b]
            remote(blocks, blocks, self.ss.at[b], self.rs.at[group, b], tensor=sib).wait_recv()

        def sent(self, b):
            blocks = self.buf.at[pl.ds(0, 7), b]
            remote(blocks, blocks, self.ss.at[b], self.rs.at[0, b], tensor=sib).wait_send()

    dy = Gather(dyf, dy_h, dy_ss, dy_rs)
    dv = Gather(dvf, None, dv_ss, dv_rs)
    own_kinds = (0, 1, 2, 3, 6)

    def to_peers(src, dst, ss, rs):
        for d in range(1, T):
            remote(src, dst, ss, rs, tensor=lax.rem(t + d, T)).start()

    def both(ref, ss, rs):
        return remote(ref, ref, ss, rs, tensor=sib)

    def e_copy(phase):
        return remote(
            ev.at[0], ev.at[1 + phase], e_ss.at[phase], e_rs.at[phase], section=partner(phase)
        )

    def ps_copy():
        return remote(p_part.at[1 - core], p_sib, xs.at[0], xs.at[1], tensor=sib)

    def dx_copy(b):
        return remote(
            dx_v.at[b], gn_h.at[b], xs.at[2], xs.at[3], section=lax.rem(s + nsec - 1, nsec)
        )

    def fold_eig(phase):
        e_copy(phase).wait()
        ev[0] = ev[0] + ev[1 + phase]

    dy.send(0, *own_kinds)
    dy.send(1, *own_kinds)

    loads[7].wait()
    ev[0] = jnp.full((1, 128), jnp.sum(eig_v[0] + eig_v[1]), F32)
    e_copy(0).start()

    for at in (0, 1, 2, 3, 4, 5, 6):
        loads[at].wait()

    def project(b, carry):
        xf = x_v[b].astype(F32)
        scaled = (xf * g_v[...]).astype(BF16)
        sqt[t, b] = jnp.sum(lanes_folded(xf * xf).T, axis=0, keepdims=True)
        part = contract(ao_v[b], fo_v[...])
        part += contract(dyf[t, b], fs_v[...])
        part += contract(scaled, fp_v[...])
        p_part[lax.rem(b, 2), b // 2] = part
        return carry

    lax.fori_loop(0, SEQS, project, 0)
    to_peers(sqt.at[t], sqt.at[t], xs.at[4], xs.at[5])
    ps_copy().start()

    def step(i, carry):
        @pl.when(i < SEQS)
        def _():
            dy.arrived(i, 0)
            dy.send(i, 4, 5)

        @pl.when(i + 2 < SEQS)
        def _():
            dy.send(i + 2, *own_kinds)

        @pl.when((i >= 1) & (i < SEQS + 1))
        def _():
            dy.arrived(i - 1, 2)
            dy.send(i - 1, 9, 10)

        @pl.when(i < SEQS)
        def _():
            dy.arrived(i, 1)
            dy.send(i, 7, 8)

        @pl.when((i >= 3) & (i < SEQS + 3))
        def _():
            dv.arrived(i - 3, 2)
            dv.send(i - 3, 9, 10)

        @pl.when((i >= 2) & (i < SEQS + 2))
        def _():
            dv.arrived(i - 2, 0)
            dv.send(i - 2, 4, 5)
            dv.arrived(i - 2, 1)
            dv.send(i - 2, 7, 8)

        @pl.when(i >= 4)
        def _():
            b = i - 4
            both(mb.at[b, pl.ds(0, T - 1)], m_ss.at[b], m_rs.at[b]).wait_recv()
            total = mb[b, 0]
            for k in range(1, T):
                total += mb[b, k]
            mean = jnp.broadcast_to(total * (1.0 / D), (LEN, 128)).T
            inv = rb[b]
            cubed = inv * inv * inv * mean
            for k in range(4):
                cols = slice(k * 128, (k + 1) * 128)
                dx = (
                    dyf[t, b, :, cols].astype(F32)
                    + inv * g_v[:, cols] * du_v[b, :, cols]
                    - x_v[b, :, cols].astype(F32) * cubed
                )
                dx_v[b, :, cols] = dx.astype(BF16)

            @pl.when(s > 0)
            def _():
                dx_copy(b).start()

        @pl.when((i >= 3) & (i < SEQS + 3))
        def _():
            b = i - 3
            dv.arrived(b, 3)
            vals = jnp.concatenate([dvf[k, b] for k in range(T)], axis=1)
            du = contract(vals, wv_v[...])
            du_v[b] = du
            cross = x_v[b].astype(F32) * g_v[...] * du
            mb[b, t] = jnp.sum(lanes_folded(cross).T, axis=0, keepdims=True)
            to_peers(mb.at[b, t], mb.at[b, t], m_ss.at[b], m_rs.at[b])

        for phase in range(phases):

            @pl.when(i == phase + 1)
            def _():
                fold_eig(phase)
                if phase + 1 < phases:
                    e_copy(phase + 1).start()

        @pl.when(i == 1)
        def _():
            for at in (8, 9, 10, 11, 12):
                loads[at].wait()
            ps_copy().wait_recv()
            for k in range(3):
                p_snd[k] = p_part[core, k] + p_sib[k]
            both(sqt.at[pl.ds(0, T - 1)], xs.at[4], xs.at[5]).wait_recv()

            def turn(b, carry):
                total = sqt[0, b]
                for k in range(1, T):
                    total += sqt[k, b]
                inv = lax.rsqrt(total * (1.0 / D) + 1e-05)
                rb[b] = jnp.broadcast_to(inv, (LEN, 128)).T
                return carry

            lax.fori_loop(0, SEQS, turn, 0)

        @pl.when(i == SEQS - 1)
        def _():
            to_peers(fvo_h.at[0], fvof.at[t, pl.ds(E, E)], xs.at[6], xs.at[7])
            for k in range(3):

                @pl.when(chip != k)
                def _():
                    slot = lax.rem(chip + 3 - k, 4)
                    remote(
                        p_snd.at[k], p_rcv.at[slot], xs.at[8], xs.at[9], tensor=2 * k + core
                    ).start()

        @pl.when((i >= 1) & (i < SEQS + 1))
        def _():
            b = i - 1
            dy.arrived(b, 3)
            acc = contract(dyf[0, b], wo_v[:, 0:W])
            for k in range(1, T):
                acc += contract(dyf[k, b], wo_v[:, k * W : (k + 1) * W])
            d_att = acc.astype(BF16)
            d_att = jnp.concatenate([d_att[:, h * HD : (h + 1) * HD] for h in range(4)], axis=0)
            probs = aw_v[b].reshape(4 * LEN, LEN)
            d_val = lax.dot_general(
                probs, d_att, (((0,), (0,)), ((), ())), preferred_element_type=F32
            )
            dvf[t, b] = d_val.astype(BF16)
            dv.send(b, *own_kinds)

        @pl.when(i == SEQS)
        def _():
            damp = ev[0] * (0.1 / (nsec * 2 * E * E))
            damp = damp[:, 0:E]
            wk[...] = jnp.zeros_like(wk)
            for m in range(2):
                under = eig_v[m] + damp
                for q in range(Q):
                    wk[m * 2 * E : m * 2 * E + E, m * 1024 + q * E : m * 1024 + (q + 1) * E] = (
                        coef_v[m, q] / under
                    )
            row = lax.broadcasted_iota(jnp.int32, (E, W), 0)
            col = lax.broadcasted_iota(jnp.int32, (E, W), 1)
            wk[E : 2 * E, W : 2 * W] = (lax.rem(col, E) == row).astype(F32)

        return carry

    lax.fori_loop(0, SEQS + 4, step, 0)

    both(fvof.at[pl.ds(0, T - 1), pl.ds(E, E)], xs.at[6], xs.at[7]).wait_recv()
    here = sc_h.at[:, pl.ds(pl.multiple_of(t * LEN, LEN), LEN)]
    keep = pltpu.make_async_copy(sc_v, here, lsem.at[14])

    @pl.when(t < SEQS)
    def _():
        both(p_rcv.at[pl.ds(0, 3)], xs.at[8], xs.at[9]).wait_recv()
        proj = p_snd[chip] + p_rcv[0] + p_rcv[1] + p_rcv[2]
        s_val = contract(dvf[0, t], fvof[0])
        for k in range(1, T):
            s_val += contract(dvf[k, t], fvof[k])
        pick = wk[:, W : 2 * W]

        def exact(left, right):
            return jnp.dot(left, right, precision=HIGH, preferred_element_type=F32)

        pairs = exact(proj, wk[:, 0:W]) * exact(proj, pick)
        pairs += exact(proj * rb[t], wk[:, 2 * W : 3 * W]) * exact(s_val, pick)
        row = lax.broadcasted_iota(jnp.int32, (Q, W), 0)
        col = lax.broadcasted_iota(jnp.int32, (Q, W), 1)
        group = (row == col // E).astype(F32)
        sc_v[...] = lax.dot_general(
            group, pairs, (((1,), (1,)), ((), ())), precision=HIGH, preferred_element_type=F32
        )
        keep.start()
        to_peers(sc_v, here, xs.at[10], xs.at[11])

    def drain(b, carry):
        dy.sent(b)
        dv.sent(b)
        both(mb.at[b, pl.ds(0, T - 1)], m_ss.at[b], m_rs.at[b]).wait_send()
        return carry

    lax.fori_loop(0, SEQS, drain, 0)
    both(sqt.at[pl.ds(0, T - 1)], xs.at[4], xs.at[5]).wait_send()
    both(fvof.at[pl.ds(0, T - 1), pl.ds(E, E)], xs.at[6], xs.at[7]).wait_send()
    ps_copy().wait_send()

    @pl.when(chip == 3)
    def _():
        both(p_snd.at[pl.ds(0, 3)], xs.at[8], xs.at[9]).wait_send()

    @pl.when(chip < 3)
    def _():
        both(p_snd.at[pl.ds(0, 2)], xs.at[8], xs.at[9]).wait_send()

    @pl.when(s > 0)
    def _():
        both(dx_v, xs.at[2], xs.at[3]).wait_send()

    @pl.when(s < nsec - 1)
    def _():
        both(gn_h, xs.at[2], xs.at[3]).wait_recv()

    @pl.when(s == nsec - 1)
    def _():
        dx_v[...] = jnp.zeros_like(dx_v)
        zero = pltpu.make_async_copy(dx_v, gn_h, lsem.at[13])
        zero.start()
        zero.wait()

    @pl.when(t < SEQS)
    def _():
        keep.wait()
        both(wk.at[pl.ds(0, Q), pl.ds(0, 7 * LEN)], xs.at[10], xs.at[11]).wait_send()
        both(sc_h.at[:, pl.ds(0, (SEQS - 1) * LEN)], xs.at[10], xs.at[11]).wait_recv()

    @pl.when(t >= SEQS)
    def _():
        both(sc_h, xs.at[10], xs.at[11]).wait_recv()


def per_device(nsec, *arrays):
    (dy, x, g, aw, ao, wv, wo, foi, foo, fvi, fvo, coef, eig) = arrays
    blocks = (SEQS, LEN, W)
    phases = nsec.bit_length() - 1
    dma = pltpu.SemaphoreType.DMA
    vmem = pltpu.VMEM
    grad_next, scores = pl.pallas_call(
        functools.partial(kernel, nsec),
        out_shape=(
            jax.ShapeDtypeStruct(blocks, BF16),
            jax.ShapeDtypeStruct((Q, SEQS * LEN), F32),
        ),
        in_specs=[pl.BlockSpec(memory_space=pltpu.HBM)] * 13,
        out_specs=(pl.BlockSpec(memory_space=pl.ANY), pl.BlockSpec(memory_space=pl.ANY)),
        scratch_shapes=[
            vmem((T, *blocks), BF16),
            vmem((T, SEQS, LEN, HD), BF16),
            vmem(blocks, BF16),
            vmem(blocks, BF16),
            vmem((SEQS, 4, LEN, LEN), BF16),
            vmem((W, 2 * W), BF16),
            vmem((W, D), BF16),
            vmem((128, W), BF16),
            vmem((128, W), BF16),
            vmem((128, W), BF16),
            vmem((T, 128, HD), BF16),
            vmem((1, W), F32),
            vmem((2, Q, E, E), F32),
            vmem((2, E, E), F32),
            vmem(blocks, F32),
            vmem(blocks, BF16),
            vmem((2, 3, LEN, 128), F32),
            vmem((3, LEN, 128), F32),
            vmem((3, LEN, 128), F32),
            vmem((3, LEN, 128), F32),
            vmem((T, SEQS, 1, 128), F32),
            vmem((SEQS, LEN, 128), F32),
            vmem((SEQS, T, 1, 128), F32),
            vmem((1 + phases, 1, 128), F32),
            vmem((128, 3 * W), F32),
            vmem((Q, LEN), F32),
            dma((15,)),
            dma((SEQS,)),
            dma((4, SEQS)),
            dma((SEQS,)),
            dma((4, SEQS)),
            dma((SEQS,)),
            dma((SEQS,)),
            dma((phases,)),
            dma((phases,)),
            dma((12,)),
        ],
        compiler_params=pltpu.CompilerParams(
            collective_id=0, has_side_effects=True, vmem_limit_bytes=LIMIT
        ),
        cost_estimate=pl.CostEstimate(
            flops=8 * 10**9, bytes_accessed=10 * 2**20, transcendentals=0
        ),
    )(
        dy.reshape(blocks),
        x.reshape(blocks),
        g,
        aw,
        ao.reshape(blocks),
        wv,
        wo,
        foi,
        foo,
        fvi,
        fvo,
        coef,
        eig,
    )
    return grad_next.reshape(SEQS * LEN, W), scores.T


def solution(mesh):
    nsec = mesh.shape["section"]
    placed = (
        P("section", "tensor"),
        P("section", "tensor"),
        P("section", "tensor"),
        P("section", None, "tensor", None, None),
        P("section", "tensor"),
        P(("section", "tensor"), None),
        P(("section", "tensor"), None),
        P("section", None, "tensor"),
        P("section", None, "tensor"),
        P("section", None, "tensor"),
        P("section", None, "tensor"),
        P("section", None, None, None, None),
        P("section", None, None, None),
    )
    return jax.shard_map(
        functools.partial(per_device, nsec),
        mesh=mesh,
        in_specs=placed,
        out_specs=(P("section", "tensor"), P("section", None)),
        check_vma=False,
    )
```

time: 106 us -> 77.2 us (0.73)
  Pallas kernels: 91.7 us -> 72.9 us
  local copies, waits for them, and re-layouts: 12.8 us -> 3.48 us
    pallas_call x1, Pallas kernels: 91.7 us -> 72.9 us  [per_device(): pl.pallas_call(functools.partial(kernel, nsec), out_shape=(jax.ShapeDtype...]
    unnamed x26 -> x2, local copies, waits for them, and re-layouts: 12.8 us -> 3.48 us
where the time goes in v2:
time: 77.2 us; the launch traced here: 77 us
  Pallas kernels  72.9 us (94%)
  local copies, waits for them, and re-layouts  3.48 us (5%)
    pallas_call x1, Pallas kernels, per_device(): pl.pallas_call(functools.partial(kernel, nsec), out_shape=(jax.ShapeDtype...  72.9 us
    unnamed x2, local copies, waits for them, and re-layouts  3.48 us

profile of v2, /device:TPU:1, one launch (start us, length us, event | category | flops | bytes accessed | tf_op | source)
XLA Modules:
  0.0 77.0 jit_solution(8664148970001863755)
XLA Ops:
  0.6 72.9 %shard_map.140 = (bf16[6,128,512]{2,1,0:T(8,128)(2,1)}, f32[16,768]{1,0:T(8,128)}) custom-call(bf16[6,128,512]{2,1,0:T(8,128)(2,1)} %bitcast.7, bf16[6,128,512]{2,1,0:T(8,128)(2,1)} %bitcast.8, f32[1,512]{1,0:T(1,128)} %g_h.1, bf16[1,6,4,128,128]{4,3,2,1,0:T(8,128)(2,1)} %aw_h.1, bf16[6,128,512]{2,1,0:T(8,128)(2,1)} %bitcast.9, bf16[512,1024]{1,0:T(8,128)(2,1)} %wv_h.1, ...), custom_call_target="tpu_custom_call" | custom-call | flops 8000000000 | bytes 10485760 | tf_op jit(solution)/shard_map/pallas_call | solution.py:450
  73.5 2.1 %copy.17 = bf16[768,512]{1,0:T(8,128)(2,1)} copy(bf16[768,512]{1,0:T(8,128)(2,1)} %bitcast.5) | data formatting | bytes 1572864
  75.6 1.4 %copy.18 = f32[768,16]{0,1:T(8,128)} copy(f32[768,16]{0,1:T(8,128)} %bitcast.6) | data formatting | bytes 98304

commit v3 on v2

--- a/solution.py
+++ b/solution.py
@@ -18,6 +18,8 @@
 HALF = LEN // 2
 MESH = pl.DeviceIdType.MESH
 LIMIT = 64_600_000
+LAST = SEQS - 1
+SLOTS = SEQS + 1
 F32 = jnp.float32
 BF16 = jnp.bfloat16
 HIGH = lax.Precision.HIGHEST
@@ -74,6 +76,11 @@
     ev,
     wk,
     sc_v,
+    zero_v,
+    aw_hi,
+    aw_lo,
+    rest_v,
+    hello,
     lsem,
     dy_ss,
     dy_rs,
@@ -130,55 +137,113 @@
         pl.semaphore_signal(
             barrier, inc=1, device_id={"tensor": lax.rem(t + d, T)}, device_id_type=MESH
         )
+
+    @pl.when(s < nsec - 1)
+    def _():
+        pl.semaphore_signal(barrier, inc=1, device_id={"section": s + 1}, device_id_type=MESH)
+
+    expected = (T - 1) + (s + nsec - 1) // nsec
     for phase in range(phases):
-        pl.semaphore_signal(
-            barrier, inc=1, device_id={"section": partner(phase)}, device_id_type=MESH
-        )
-    pl.semaphore_signal(
-        barrier, inc=1, device_id={"section": lax.rem(s + 1, nsec)}, device_id_type=MESH
-    )
+        upper = lax.rem(s // 2**phase, 2)
+        expected += upper
+
+        @pl.when(upper == 0)
+        def _():
+            pl.semaphore_signal(
+                barrier, inc=1, device_id={"section": partner(phase)}, device_id_type=MESH
+            )
+
     for load in loads:
         load.start()
-    pl.semaphore_wait(barrier, (T - 1) + phases + 1)
-
-    low, high, whole = pl.ds(0, HALF), pl.ds(HALF, HALF), pl.ds(0, LEN)
-    routes = [
-        (t, low, right, 0),
-        (t, high, left, 0),
-        (t, high, right, 1),
-        (t, low, left, 1),
-        (left, low, right, 2),
-        (right, high, left, 2),
-        (t, whole, sib, 3),
-        (left, whole, sib, 3),
-        (right, whole, sib, 3),
-        (across, low, sib, 3),
-        (across, high, sib, 3),
-    ]
+    pl.semaphore_wait(barrier, expected)
+    for phase in range(phases):
+
+        @pl.when(lax.rem(s // 2**phase, 2) == 1)
+        def _():
+            pl.semaphore_signal(
+                hello.at[phase], inc=1, device_id={"section": partner(phase)}, device_id_type=MESH
+            )
+
+    def ring_routes(first, count):
+        half = count // 2
+        low, high = pl.ds(first, half), pl.ds(first + half, half)
+        whole = pl.ds(first, count)
+        return [
+            (t, low, right, 0),
+            (t, high, left, 0),
+            (t, high, right, 1),
+            (t, low, left, 1),
+            (left, low, right, 2),
+            (right, high, left, 2),
+            (t, whole, sib, 3),
+            (left, whole, sib, 3),
+            (right, whole, sib, 3),
+            (across, low, sib, 3),
+            (across, high, sib, 3),
+        ]
+
+    def short_routes(first, count):
+        whole = pl.ds(first, count)
+        return [
+            (t, whole, right, 0),
+            (t, whole, left, 0),
+            (t, whole, across, 1),
+            (t, whole, sib, 3),
+            (left, whole, sib, 3),
+            (right, whole, sib, 3),
+            (across, whole, sib, 3),
+        ]
 
     class Gather:
-        def __init__(self, buf, own, ss, rs):
-            self.buf, self.own, self.ss, self.rs = buf, own, ss, rs
-
-        def send(self, b, *kinds):
+        def __init__(self, buf, own, ss, rs, slot, b, first, count, routes):
+            self.buf, self.own, self.slot = buf, own, slot
+            self.ss, self.rs = ss, rs
+            self.b, self.rows, self.routes = b, pl.ds(first, count), routes
+
+        def send(self, *kinds):
             for kind in kinds:
-                source, rows, target, group = routes[kind]
-                dst = self.buf.at[source, b, rows]
+                source, rows, target, group = self.routes[kind]
+                dst = self.buf.at[source, self.b, rows]
                 src = dst
-                if self.own is not None and kind in (0, 1, 2, 3, 6):
-                    src = self.own.at[b, rows]
-                remote(src, dst, self.ss.at[b], self.rs.at[group, b], tensor=target).start()
-
-        def arrived(self, b, group):
-            blocks = self.buf.at[pl.ds(0, 4 if group == 3 else 1), b]
-            remote(blocks, blocks, self.ss.at[b], self.rs.at[group, b], tensor=sib).wait_recv()
-
-        def sent(self, b):
-            blocks = self.buf.at[pl.ds(0, 7), b]
-            remote(blocks, blocks, self.ss.at[b], self.rs.at[0, b], tensor=sib).wait_send()
-
-    dy = Gather(dyf, dy_h, dy_ss, dy_rs)
-    dv = Gather(dvf, None, dv_ss, dv_rs)
+                if self.own is not None and source is t:
+                    src = self.own.at[self.b, rows]
+                remote(
+                    src, dst, self.ss.at[self.slot], self.rs.at[group, self.slot], tensor=target
+                ).start()
+
+        def blocks(self, count, group):
+            ref = self.buf.at[pl.ds(0, count), self.b, self.rows]
+            return remote(
+                ref, ref, self.ss.at[self.slot], self.rs.at[group, self.slot], tensor=sib
+            )
+
+        def arrived(self, group, count=1):
+            self.blocks(count, group).wait_recv()
+
+        def sent(self):
+            self.blocks(7, 0).wait_send()
+
+        def spread(self):
+            for d in range(1, T):
+                ref = self.buf.at[t, self.b, self.rows]
+                remote(
+                    ref,
+                    ref,
+                    self.ss.at[self.slot],
+                    self.rs.at[3, self.slot],
+                    tensor=lax.rem(t + d, T),
+                ).start()
+
+    def dy(b):
+        return Gather(dyf, dy_h, dy_ss, dy_rs, b, b, 0, LEN, ring_routes(0, LEN))
+
+    def dv(b):
+        return Gather(dvf, None, dv_ss, dv_rs, b, b, 0, LEN, ring_routes(0, LEN))
+
+    dy_hi = Gather(dyf, dy_h, dy_ss, dy_rs, LAST, LAST, HALF, HALF, ring_routes(HALF, HALF))
+    dy_lo = Gather(dyf, dy_h, dy_ss, dy_rs, SEQS, LAST, 0, HALF, short_routes(0, HALF))
+    dv_hi = Gather(dvf, None, dv_ss, dv_rs, LAST, LAST, HALF, HALF, None)
+    dv_lo = Gather(dvf, None, dv_ss, dv_rs, SEQS, LAST, 0, HALF, None)
     own_kinds = (0, 1, 2, 3, 6)
 
     def to_peers(src, dst, ss, rs):
@@ -196,21 +261,33 @@
     def ps_copy():
         return remote(p_part.at[1 - core], p_sib, xs.at[0], xs.at[1], tensor=sib)
 
-    def dx_copy(b):
+    def dx_copy(b, rows):
         return remote(
-            dx_v.at[b], gn_h.at[b], xs.at[2], xs.at[3], section=lax.rem(s + nsec - 1, nsec)
+            dx_v.at[b, rows],
+            gn_h.at[b, rows],
+            xs.at[2],
+            xs.at[3],
+            section=lax.rem(s + nsec - 1, nsec),
         )
+
+    zero = pltpu.make_async_copy(zero_v, gn_h, lsem.at[13])
+
+    def start_eig(phase):
+        @pl.when(lax.rem(s // 2**phase, 2) == 0)
+        def _():
+            pl.semaphore_wait(hello.at[phase], 1)
+
+        e_copy(phase).start()
 
     def fold_eig(phase):
         e_copy(phase).wait()
         ev[0] = ev[0] + ev[1 + phase]
 
-    dy.send(0, *own_kinds)
-    dy.send(1, *own_kinds)
+    dy(0).send(*own_kinds)
+    dy(1).send(*own_kinds)
 
     loads[7].wait()
     ev[0] = jnp.full((1, 128), jnp.sum(eig_v[0] + eig_v[1]), F32)
-    e_copy(0).start()
 
     for at in (0, 1, 2, 3, 4, 5, 6):
         loads[at].wait()
@@ -229,79 +306,111 @@
     to_peers(sqt.at[t], sqt.at[t], xs.at[4], xs.at[5])
     ps_copy().start()
 
+    @pl.when(s == nsec - 1)
+    def _():
+        zero_v[...] = jnp.zeros_like(zero_v)
+        zero.start()
+
+    def value_grad(b):
+        dy(b).arrived(3, 4)
+        acc = contract(wo_v[:, 0:W], dyf[0, b])
+        for k in range(1, T):
+            acc += contract(wo_v[:, k * W : (k + 1) * W], dyf[k, b])
+        d_att = acc.astype(BF16)
+        d_att = jnp.concatenate([d_att[h * HD : (h + 1) * HD] for h in range(4)], axis=1)
+        probs = aw_v[b].reshape(4 * LEN, LEN)
+        d_val = jnp.dot(d_att, probs, preferred_element_type=F32).T
+        dvf[t, b] = d_val.astype(BF16)
+        dv(b).send(*own_kinds)
+
+    def half_terms(first, probs):
+        rows = pl.ds(first, HALF)
+        acc = contract(dyf[0, LAST, rows], wo_v[:, 0:W])
+        for k in range(1, T):
+            acc += contract(dyf[k, LAST, rows], wo_v[:, k * W : (k + 1) * W])
+        d_att = acc.astype(BF16)
+        d_att = jnp.concatenate([d_att[:, h * HD : (h + 1) * HD] for h in range(4)], axis=0)
+        return jnp.dot(probs, d_att, preferred_element_type=F32)
+
+    def input_grad(slot, b, first, count):
+        rows = pl.ds(first, count)
+        vals = jnp.concatenate([dvf[k, b, rows] for k in range(T)], axis=1)
+        du = contract(vals, wv_v[...])
+        du_v[b, rows] = du
+        cross = lanes_folded(x_v[b, rows].astype(F32) * g_v[...] * du)
+        if count < LEN:
+            cross = jnp.concatenate([cross, jnp.zeros((LEN - count, 128), F32)], axis=0)
+        mb[slot, t] = jnp.sum(cross.T, axis=0, keepdims=True)
+        to_peers(mb.at[slot, t], mb.at[slot, t], m_ss.at[slot], m_rs.at[slot])
+
+    def relay(slot, b, first, count):
+        rows = pl.ds(first, count)
+        both(mb.at[slot, pl.ds(0, T - 1)], m_ss.at[slot], m_rs.at[slot]).wait_recv()
+        total = mb[slot, 0]
+        for k in range(1, T):
+            total += mb[slot, k]
+        mean = jnp.broadcast_to(total * (1.0 / D), (LEN, 128)).T[0:count]
+        inv = rb[b, rows]
+        cubed = inv * inv * inv * mean
+        for k in range(4):
+            cols = slice(k * 128, (k + 1) * 128)
+            dx = (
+                dyf[t, b, rows, cols].astype(F32)
+                + inv * g_v[:, cols] * du_v[b, rows, cols]
+                - x_v[b, rows, cols].astype(F32) * cubed
+            )
+            dx_v[b, rows, cols] = dx.astype(BF16)
+
+        @pl.when(s > 0)
+        def _():
+            dx_copy(b, rows).start()
+
+    def forward_vals(b):
+        dv(b).arrived(0)
+        dv(b).send(4, 5)
+        dv(b).arrived(1)
+        dv(b).send(7, 8)
+
+    def finish_vals(b):
+        dv(b).arrived(2)
+        dv(b).send(9, 10)
+
     def step(i, carry):
-        @pl.when(i < SEQS)
-        def _():
-            dy.arrived(i, 0)
-            dy.send(i, 4, 5)
-
-        @pl.when(i + 2 < SEQS)
-        def _():
-            dy.send(i + 2, *own_kinds)
-
-        @pl.when((i >= 1) & (i < SEQS + 1))
-        def _():
-            dy.arrived(i - 1, 2)
-            dy.send(i - 1, 9, 10)
-
-        @pl.when(i < SEQS)
-        def _():
-            dy.arrived(i, 1)
-            dy.send(i, 7, 8)
-
-        @pl.when((i >= 3) & (i < SEQS + 3))
-        def _():
-            dv.arrived(i - 3, 2)
-            dv.send(i - 3, 9, 10)
-
-        @pl.when((i >= 2) & (i < SEQS + 2))
-        def _():
-            dv.arrived(i - 2, 0)
-            dv.send(i - 2, 4, 5)
-            dv.arrived(i - 2, 1)
-            dv.send(i - 2, 7, 8)
+        dy(i).arrived(0)
+        dy(i).send(4, 5)
+
+        @pl.when(i >= 1)
+        def _():
+            dy(i - 1).arrived(2)
+            dy(i - 1).send(9, 10)
+
+        dy(i).arrived(1)
+        dy(i).send(7, 8)
+
+        @pl.when(i >= 3)
+        def _():
+            finish_vals(i - 3)
+
+        @pl.when(i >= 2)
+        def _():
+            forward_vals(i - 2)
 
         @pl.when(i >= 4)
         def _():
-            b = i - 4
-            both(mb.at[b, pl.ds(0, T - 1)], m_ss.at[b], m_rs.at[b]).wait_recv()
-            total = mb[b, 0]
-            for k in range(1, T):
-                total += mb[b, k]
-            mean = jnp.broadcast_to(total * (1.0 / D), (LEN, 128)).T
-            inv = rb[b]
-            cubed = inv * inv * inv * mean
-            for k in range(4):
-                cols = slice(k * 128, (k + 1) * 128)
-                dx = (
-                    dyf[t, b, :, cols].astype(F32)
-                    + inv * g_v[:, cols] * du_v[b, :, cols]
-                    - x_v[b, :, cols].astype(F32) * cubed
-                )
-                dx_v[b, :, cols] = dx.astype(BF16)
-
-            @pl.when(s > 0)
+            relay(i - 4, i - 4, 0, LEN)
+
+        @pl.when(i >= 3)
+        def _():
+            dv(i - 3).arrived(3, 4)
+            input_grad(i - 3, i - 3, 0, LEN)
+
+        for phase in range(phases):
+
+            @pl.when(i == phase)
             def _():
-                dx_copy(b).start()
-
-        @pl.when((i >= 3) & (i < SEQS + 3))
-        def _():
-            b = i - 3
-            dv.arrived(b, 3)
-            vals = jnp.concatenate([dvf[k, b] for k in range(T)], axis=1)
-            du = contract(vals, wv_v[...])
-            du_v[b] = du
-            cross = x_v[b].astype(F32) * g_v[...] * du
-            mb[b, t] = jnp.sum(lanes_folded(cross).T, axis=0, keepdims=True)
-            to_peers(mb.at[b, t], mb.at[b, t], m_ss.at[b], m_rs.at[b])
-
-        for phase in range(phases):
-
-            @pl.when(i == phase + 1)
-            def _():
-                fold_eig(phase)
-                if phase + 1 < phases:
-                    e_copy(phase + 1).start()
+                if phase > 0:
+                    fold_eig(phase - 1)
+                start_eig(phase)
 
         @pl.when(i == 1)
         def _():
@@ -321,53 +430,97 @@
                 return carry
 
             lax.fori_loop(0, SEQS, turn, 0)
-
-        @pl.when(i == SEQS - 1)
-        def _():
-            to_peers(fvo_h.at[0], fvof.at[t, pl.ds(E, E)], xs.at[6], xs.at[7])
-            for k in range(3):
-
-                @pl.when(chip != k)
-                def _():
-                    slot = lax.rem(chip + 3 - k, 4)
-                    remote(
-                        p_snd.at[k], p_rcv.at[slot], xs.at[8], xs.at[9], tensor=2 * k + core
-                    ).start()
-
-        @pl.when((i >= 1) & (i < SEQS + 1))
-        def _():
-            b = i - 1
-            dy.arrived(b, 3)
-            acc = contract(dyf[0, b], wo_v[:, 0:W])
-            for k in range(1, T):
-                acc += contract(dyf[k, b], wo_v[:, k * W : (k + 1) * W])
-            d_att = acc.astype(BF16)
-            d_att = jnp.concatenate([d_att[:, h * HD : (h + 1) * HD] for h in range(4)], axis=0)
-            probs = aw_v[b].reshape(4 * LEN, LEN)
-            d_val = lax.dot_general(
-                probs, d_att, (((0,), (0,)), ((), ())), preferred_element_type=F32
+            aw_hi[...] = aw_v[LAST, :, HALF:LEN].reshape(4 * HALF, LEN).T
+            aw_lo[...] = aw_v[LAST, :, 0:HALF].reshape(4 * HALF, LEN).T
+
+        @pl.when(i >= 1)
+        def _():
+            value_grad(i - 1)
+
+        @pl.when(i + 2 < LAST)
+        def _():
+            dy(i + 2).send(*own_kinds)
+
+        @pl.when(i + 2 == LAST)
+        def _():
+            dy_hi.send(*own_kinds)
+
+        @pl.when(i + 1 == LAST)
+        def _():
+            dy_lo.send(0, 1, 2, 3)
+
+        return carry
+
+    lax.fori_loop(0, LAST, step, 0)
+
+    dy_hi.arrived(0)
+    dy_hi.send(4, 5)
+    dy(LAST - 1).arrived(2)
+    dy(LAST - 1).send(9, 10)
+    dy_hi.arrived(1)
+    dy_hi.send(7, 8)
+    finish_vals(LAST - 3)
+    forward_vals(LAST - 2)
+    relay(LAST - 4, LAST - 4, 0, LEN)
+    dv(LAST - 3).arrived(3, 4)
+    input_grad(LAST - 3, LAST - 3, 0, LEN)
+    value_grad(LAST - 1)
+
+    dy_lo.arrived(0, 2)
+    dy_lo.send(4, 5)
+    dy_hi.arrived(2)
+    dy_hi.send(9, 10)
+    dy_lo.arrived(1)
+    dy_lo.send(6)
+    to_peers(fvo_h.at[0], fvof.at[t, pl.ds(E, E)], xs.at[6], xs.at[7])
+    for k in range(3):
+
+        @pl.when(chip != k)
+        def _():
+            slot = lax.rem(chip + 3 - k, 4)
+            remote(p_snd.at[k], p_rcv.at[slot], xs.at[8], xs.at[9], tensor=2 * k + core).start()
+
+    dy_hi.arrived(3, 4)
+    terms = half_terms(HALF, aw_hi[...])
+    rest_v[...] = terms[0:HALF]
+    dvf[t, LAST, pl.ds(HALF, HALF)] = terms[HALF:LEN].astype(BF16)
+    dv_hi.spread()
+
+    dy_lo.arrived(3, 4)
+    terms = half_terms(0, aw_lo[0:HALF])
+    dvf[t, LAST, pl.ds(0, HALF)] = (terms + rest_v[...]).astype(BF16)
+    dv_lo.spread()
+
+    forward_vals(LAST - 1)
+    finish_vals(LAST - 2)
+    relay(LAST - 3, LAST - 3, 0, LEN)
+    dv(LAST - 2).arrived(3, 4)
+    input_grad(LAST - 2, LAST - 2, 0, LEN)
+    finish_vals(LAST - 1)
+    dv_hi.arrived(3, 7)
+    input_grad(LAST, LAST, HALF, HALF)
+    dv(LAST - 1).arrived(3, 4)
+    input_grad(LAST - 1, LAST - 1, 0, LEN)
+    dv_lo.arrived(3, 7)
+    input_grad(SEQS, LAST, 0, HALF)
+    relay(LAST - 2, LAST - 2, 0, LEN)
+    relay(LAST - 1, LAST - 1, 0, LEN)
+    relay(LAST, LAST, HALF, HALF)
+    relay(SEQS, LAST, 0, HALF)
+
+    fold_eig(phases - 1)
+    damp = ev[0] * (0.1 / (nsec * 2 * E * E))
+    damp = damp[:, 0:E]
+    wk[...] = jnp.zeros_like(wk)
+    for m in range(2):
+        under = eig_v[m] + damp
+        for q in range(Q):
+            wk[m * 2 * E : m * 2 * E + E, m * 1024 + q * E : m * 1024 + (q + 1) * E] = (
+                coef_v[m, q] / under
             )
-            dvf[t, b] = d_val.astype(BF16)
-            dv.send(b, *own_kinds)
-
-        @pl.when(i == SEQS)
-        def _():
-            damp = ev[0] * (0.1 / (nsec * 2 * E * E))
-            damp = damp[:, 0:E]
-            wk[...] = jnp.zeros_like(wk)
-            for m in range(2):
-                under = eig_v[m] + damp
-                for q in range(Q):
-                    wk[m * 2 * E : m * 2 * E + E, m * 1024 + q * E : m * 1024 + (q + 1) * E] = (
-                        coef_v[m, q] / under
-                    )
-            row = lax.broadcasted_iota(jnp.int32, (E, W), 0)
-            col = lax.broadcasted_iota(jnp.int32, (E, W), 1)
-            wk[E : 2 * E, W : 2 * W] = (lax.rem(col, E) == row).astype(F32)
-
-        return carry
-
-    lax.fori_loop(0, SEQS + 4, step, 0)
+    row = lax.broadcasted_iota(jnp.int32, (E, W), 0)
+    col = lax.broadcasted_iota(jnp.int32, (E, W), 1)
+    wk[E : 2 * E, W : 2 * W] = (lax.rem(col, E) == row).astype(F32)
 
     both(fvof.at[pl.ds(0, T - 1), pl.ds(E, E)], xs.at[6], xs.at[7]).wait_recv()
     here = sc_h.at[:, pl.ds(pl.multiple_of(t * LEN, LEN), LEN)]
@@ -397,12 +550,18 @@
         to_peers(sc_v, here, xs.at[10], xs.at[11])
 
     def drain(b, carry):
-        dy.sent(b)
-        dv.sent(b)
-        both(mb.at[b, pl.ds(0, T - 1)], m_ss.at[b], m_rs.at[b]).wait_send()
+        dy(b).sent()
+        dv(b).sent()
         return carry
 
-    lax.fori_loop(0, SEQS, drain, 0)
+    def drain_sums(slot, carry):
+        both(mb.at[slot, pl.ds(0, T - 1)], m_ss.at[slot], m_rs.at[slot]).wait_send()
+        return carry
+
+    lax.fori_loop(0, LAST, drain, 0)
+    lax.fori_loop(0, SLOTS, drain_sums, 0)
+    for gather in (dy_hi, dy_lo, dv_hi, dv_lo):
+        gather.sent()
     both(sqt.at[pl.ds(0, T - 1)], xs.at[4], xs.at[5]).wait_send()
     both(fvof.at[pl.ds(0, T - 1), pl.ds(E, E)], xs.at[6], xs.at[7]).wait_send()
     ps_copy().wait_send()
@@ -425,9 +584,6 @@
 
     @pl.when(s == nsec - 1)
     def _():
-        dx_v[...] = jnp.zeros_like(dx_v)
-        zero = pltpu.make_async_copy(dx_v, gn_h, lsem.at[13])
-        zero.start()
         zero.wait()
 
     @pl.when(t < SEQS)
@@ -439,6 +595,24 @@
     @pl.when(t >= SEQS)
     def _():
         both(sc_h, xs.at[10], xs.at[11]).wait_recv()
+
+
+def hand_over(gn_h, sc_h, gn_o, sc_o, gn_v, sc_v, in_sem, out_sem):
+    pieces = [(gn_h.at[b], gn_v.at[b], gn_o.at[b]) for b in range(SEQS)]
+    pieces.append((sc_h, sc_v, sc_o))
+    inward = [
+        pltpu.make_async_copy(src, mid, in_sem.at[k]) for k, (src, mid, dst) in enumerate(pieces)
+    ]
+    outward = [
+        pltpu.make_async_copy(mid, dst, out_sem.at[k]) for k, (src, mid, dst) in enumerate(pieces)
+    ]
+    for copy in inward:
+        copy.start()
+    for first, second in zip(inward, outward):
+        first.wait()
+        second.start()
+    for copy in outward:
+        copy.wait()
 
 
 def per_device(nsec, *arrays):
@@ -478,17 +652,22 @@
             vmem((3, LEN, 128), F32),
             vmem((T, SEQS, 1, 128), F32),
             vmem((SEQS, LEN, 128), F32),
-            vmem((SEQS, T, 1, 128), F32),
+            vmem((SLOTS, T, 1, 128), F32),
             vmem((1 + phases, 1, 128), F32),
             vmem((128, 3 * W), F32),
             vmem((Q, LEN), F32),
+            vmem(blocks, BF16),
+            vmem((LEN, 4 * HALF), BF16),
+            vmem((LEN, 4 * HALF), BF16),
+            vmem((HALF, HD), F32),
+            pltpu.SemaphoreType.REGULAR((phases,)),
             dma((15,)),
-            dma((SEQS,)),
-            dma((4, SEQS)),
-            dma((SEQS,)),
-            dma((4, SEQS)),
-            dma((SEQS,)),
-            dma((SEQS,)),
+            dma((SLOTS,)),
+            dma((4, SLOTS)),
+            dma((SLOTS,)),
+            dma((4, SLOTS)),
+            dma((SLOTS,)),
+            dma((SLOTS,)),
             dma((phases,)),
             dma((phases,)),
             dma((12,)),
@@ -514,6 +693,22 @@
         coef,
         eig,
     )
+    grad_next, scores = pl.pallas_call(
+        hand_over,
+        out_shape=(
+            jax.ShapeDtypeStruct(blocks, BF16),
+            jax.ShapeDtypeStruct((Q, SEQS * LEN), F32),
+        ),
+        in_specs=[pl.BlockSpec(memory_space=pl.ANY)] * 2,
+        out_specs=(pl.BlockSpec(memory_space=pl.ANY), pl.BlockSpec(memory_space=pl.ANY)),
+        scratch_shapes=[
+            vmem(blocks, BF16),
+            vmem((Q, SEQS * LEN), F32),
+            dma((SEQS + 1,)),
+            dma((SEQS + 1,)),
+        ],
+        compiler_params=pltpu.CompilerParams(vmem_limit_bytes=LIMIT),
+    )(grad_next, scores)
     return grad_next.reshape(SEQS * LEN, W), scores.T
 
 

time: 77.2 us -> 68.4 us (0.89)
  the two profiles are of different devices: /device:TPU:1 before, /device:TPU:102 now
where the time goes in v3:
time: 68.4 us; the launch traced here: 68.3 us
  Pallas kernels  67.7 us (99%)
    pallas_call x1, Pallas kernels, per_device(): pl.pallas_call(functools.partial(kernel, nsec), out_shape=(jax.ShapeDtype...  65.7 us
    pallas_call x1, Pallas kernels, per_device(): pl.pallas_call(hand_over, out_shape=(jax.ShapeDtypeStruct(blocks, BF16),...  1.99 us

profile of v3, /device:TPU:102, one launch (start us, length us, event | category | flops | bytes accessed | tf_op | source)
XLA Modules:
  0.0 68.3 jit_solution(12867695373258844698)
XLA Ops:
  0.6 65.7 %shard_map.140 = (bf16[6,128,512]{2,1,0:T(8,128)(2,1)}, f32[16,768]{1,0:T(8,128)}) custom-call(bf16[6,128,512]{2,1,0:T(8,128)(2,1)} %bitcast.5, bf16[6,128,512]{2,1,0:T(8,128)(2,1)} %bitcast.6, f32[1,512]{1,0:T(1,128)} %g_h.1, bf16[1,6,4,128,128]{4,3,2,1,0:T(8,128)(2,1)} %aw_h.1, bf16[6,128,512]{2,1,0:T(8,128)(2,1)} %bitcast.7, bf16[512,1024]{1,0:T(8,128)(2,1)} %wv_h.1, ...), custom_call_target="tpu_custom_call" | custom-call | flops 8000000000 | bytes 10485760 | tf_op jit(solution)/shard_map/pallas_call | solution.py:624
  66.3 2.0 %shard_map.141 = (bf16[6,128,512]{2,1,0:T(8,128)(2,1)}, f32[16,768]{1,0:T(8,128)}) custom-call(bf16[6,128,512]{2,1,0:T(8,128)(2,1)} %get-tuple-element.6.gn_h, f32[16,768]{1,0:T(8,128)} %get-tuple-element.7.sc_h), custom_call_target="tpu_custom_call" | custom-call | tf_op jit(solution)/shard_map/pallas_call | solution.py:696

commit v4 on v3

--- a/solution.py
+++ b/solution.py
@@ -238,13 +238,14 @@
         return Gather(dyf, dy_h, dy_ss, dy_rs, b, b, 0, LEN, ring_routes(0, LEN))
 
     def dv(b):
-        return Gather(dvf, None, dv_ss, dv_rs, b, b, 0, LEN, ring_routes(0, LEN))
+        return Gather(dvf, None, dv_ss, dv_rs, b, b, 0, LEN, short_routes(0, LEN))
 
     dy_hi = Gather(dyf, dy_h, dy_ss, dy_rs, LAST, LAST, HALF, HALF, ring_routes(HALF, HALF))
     dy_lo = Gather(dyf, dy_h, dy_ss, dy_rs, SEQS, LAST, 0, HALF, short_routes(0, HALF))
-    dv_hi = Gather(dvf, None, dv_ss, dv_rs, LAST, LAST, HALF, HALF, None)
-    dv_lo = Gather(dvf, None, dv_ss, dv_rs, SEQS, LAST, 0, HALF, None)
+    dv_hi = Gather(dvf, None, dv_ss, dv_rs, LAST, LAST, HALF, HALF, short_routes(HALF, HALF))
+    dv_lo = Gather(dvf, None, dv_ss, dv_rs, SEQS, LAST, 0, HALF, short_routes(0, HALF))
     own_kinds = (0, 1, 2, 3, 6)
+    short_kinds = (2, 0, 1, 3)
 
     def to_peers(src, dst, ss, rs):
         for d in range(1, T):
@@ -321,7 +322,7 @@
         probs = aw_v[b].reshape(4 * LEN, LEN)
         d_val = jnp.dot(d_att, probs, preferred_element_type=F32).T
         dvf[t, b] = d_val.astype(BF16)
-        dv(b).send(*own_kinds)
+        dv(b).send(*short_kinds)
 
     def half_terms(first, probs):
         rows = pl.ds(first, HALF)
@@ -365,15 +366,11 @@
         def _():
             dx_copy(b, rows).start()
 
-    def forward_vals(b):
-        dv(b).arrived(0)
-        dv(b).send(4, 5)
-        dv(b).arrived(1)
-        dv(b).send(7, 8)
-
-    def finish_vals(b):
-        dv(b).arrived(2)
-        dv(b).send(9, 10)
+    def share_vals(gather):
+        gather.arrived(0, 2)
+        gather.send(4, 5)
+        gather.arrived(1)
+        gather.send(6)
 
     def step(i, carry):
         dy(i).arrived(0)
@@ -386,18 +383,6 @@
 
         dy(i).arrived(1)
         dy(i).send(7, 8)
-
-        @pl.when(i >= 3)
-        def _():
-            finish_vals(i - 3)
-
-        @pl.when(i >= 2)
-        def _():
-            forward_vals(i - 2)
-
-        @pl.when(i >= 4)
-        def _():
-            relay(i - 4, i - 4, 0, LEN)
 
         @pl.when(i >= 3)
         def _():
@@ -419,6 +404,25 @@
             ps_copy().wait_recv()
             for k in range(3):
                 p_snd[k] = p_part[core, k] + p_sib[k]
+
+        @pl.when(i >= 1)
+        def _():
+            value_grad(i - 1)
+
+        @pl.when(i + 2 < LAST)
+        def _():
+            dy(i + 2).send(*own_kinds)
+
+        @pl.when(i + 2 == LAST)
+        def _():
+            dy_hi.send(*own_kinds)
+
+        @pl.when(i + 1 == LAST)
+        def _():
+            dy_lo.send(0, 1, 2, 3)
+
+        @pl.when(i == 2)
+        def _():
             both(sqt.at[pl.ds(0, T - 1)], xs.at[4], xs.at[5]).wait_recv()
 
             def turn(b, carry):
@@ -433,21 +437,13 @@
             aw_hi[...] = aw_v[LAST, :, HALF:LEN].reshape(4 * HALF, LEN).T
             aw_lo[...] = aw_v[LAST, :, 0:HALF].reshape(4 * HALF, LEN).T
 
-        @pl.when(i >= 1)
-        def _():
-            value_grad(i - 1)
-
-        @pl.when(i + 2 < LAST)
-        def _():
-            dy(i + 2).send(*own_kinds)
-
-        @pl.when(i + 2 == LAST)
-        def _():
-            dy_hi.send(*own_kinds)
-
-        @pl.when(i + 1 == LAST)
-        def _():
-            dy_lo.send(0, 1, 2, 3)
+        @pl.when(i >= 2)
+        def _():
+            share_vals(dv(i - 2))
+
+        @pl.when(i >= 3)
+        def _():
+            relay(i - 3, i - 3, 0, LEN)
 
         return carry
 
@@ -459,9 +455,6 @@
     dy(LAST - 1).send(9, 10)
     dy_hi.arrived(1)
     dy_hi.send(7, 8)
-    finish_vals(LAST - 3)
-    forward_vals(LAST - 2)
-    relay(LAST - 4, LAST - 4, 0, LEN)
     dv(LAST - 3).arrived(3, 4)
     input_grad(LAST - 3, LAST - 3, 0, LEN)
     value_grad(LAST - 1)
@@ -470,40 +463,43 @@
     dy_lo.send(4, 5)
     dy_hi.arrived(2)
     dy_hi.send(9, 10)
+    share_vals(dv(LAST - 2))
     dy_lo.arrived(1)
     dy_lo.send(6)
+    relay(LAST - 3, LAST - 3, 0, LEN)
     to_peers(fvo_h.at[0], fvof.at[t, pl.ds(E, E)], xs.at[6], xs.at[7])
     for k in range(3):
 
         @pl.when(chip != k)
         def _():
             slot = lax.rem(chip + 3 - k, 4)
-            remote(p_snd.at[k], p_rcv.at[slot], xs.at[8], xs.at[9], tensor=2 * k + core).start()
+            remote(
+                p_snd.at[k], p_rcv.at[slot], xs.at[8], xs.at[9], tensor=2 * k + core
+            ).start()
 
     dy_hi.arrived(3, 4)
     terms = half_terms(HALF, aw_hi[...])
     rest_v[...] = terms[0:HALF]
     dvf[t, LAST, pl.ds(HALF, HALF)] = terms[HALF:LEN].astype(BF16)
-    dv_hi.spread()
+    dv_hi.send(*short_kinds)
+    dv(LAST - 2).arrived(3, 4)
+    input_grad(LAST - 2, LAST - 2, 0, LEN)
 
     dy_lo.arrived(3, 4)
     terms = half_terms(0, aw_lo[0:HALF])
     dvf[t, LAST, pl.ds(0, HALF)] = (terms + rest_v[...]).astype(BF16)
-    dv_lo.spread()
-
-    forward_vals(LAST - 1)
-    finish_vals(LAST - 2)
-    relay(LAST - 3, LAST - 3, 0, LEN)
-    dv(LAST - 2).arrived(3, 4)
-    input_grad(LAST - 2, LAST - 2, 0, LEN)
-    finish_vals(LAST - 1)
-    dv_hi.arrived(3, 7)
-    input_grad(LAST, LAST, HALF, HALF)
+    dv_lo.send(*short_kinds)
+
+    share_vals(dv(LAST - 1))
+    share_vals(dv_hi)
+    relay(LAST - 2, LAST - 2, 0, LEN)
     dv(LAST - 1).arrived(3, 4)
     input_grad(LAST - 1, LAST - 1, 0, LEN)
-    dv_lo.arrived(3, 7)
+    share_vals(dv_lo)
+    dv_hi.arrived(3, 4)
+    input_grad(LAST, LAST, HALF, HALF)
+    dv_lo.arrived(3, 4)
     input_grad(SEQS, LAST, 0, HALF)
-    relay(LAST - 2, LAST - 2, 0, LEN)
     relay(LAST - 1, LAST - 1, 0, LEN)
     relay(LAST, LAST, HALF, HALF)
     relay(SEQS, LAST, 0, HALF)

time: 68.4 us -> 65.6 us (0.959)
  Pallas kernels: 67.7 us -> 64.8 us
    pallas_call x1, Pallas kernels: 65.7 us -> 62.8 us  [per_device(): pl.pallas_call(functools.partial(kernel, nsec), out_shape=(jax.ShapeDtype...]
where the time goes in v4:
time: 65.6 us; the launch traced here: 65.5 us
  Pallas kernels  64.8 us (99%)
    pallas_call x1, Pallas kernels, per_device(): pl.pallas_call(functools.partial(kernel, nsec), out_shape=(jax.ShapeDtype...  62.8 us
    pallas_call x1, Pallas kernels, per_device(): pl.pallas_call(hand_over, out_shape=(jax.ShapeDtypeStruct(blocks, BF16),...  1.99 us

profile of v4, /device:TPU:102, one launch (start us, length us, event | category | flops | bytes accessed | tf_op | source)
XLA Modules:
  0.0 65.5 jit_solution(5374160155021599335)
XLA Ops:
  0.6 62.8 %shard_map.140 = (bf16[6,128,512]{2,1,0:T(8,128)(2,1)}, f32[16,768]{1,0:T(8,128)}) custom-call(bf16[6,128,512]{2,1,0:T(8,128)(2,1)} %bitcast.5, bf16[6,128,512]{2,1,0:T(8,128)(2,1)} %bitcast.6, f32[1,512]{1,0:T(1,128)} %g_h.1, bf16[1,6,4,128,128]{4,3,2,1,0:T(8,128)(2,1)} %aw_h.1, bf16[6,128,512]{2,1,0:T(8,128)(2,1)} %bitcast.7, bf16[512,1024]{1,0:T(8,128)(2,1)} %wv_h.1, ...), custom_call_target="tpu_custom_call" | custom-call | flops 8000000000 | bytes 10485760 | tf_op jit(solution)/shard_map/pallas_call | solution.py:620
  63.5 2.0 %shard_map.141 = (bf16[6,128,512]{2,1,0:T(8,128)(2,1)}, f32[16,768]{1,0:T(8,128)}) custom-call(bf16[6,128,512]{2,1,0:T(8,128)(2,1)} %get-tuple-element.6.gn_h, f32[16,768]{1,0:T(8,128)} %get-tuple-element.7.sc_h), custom_call_target="tpu_custom_call" | custom-call | tf_op jit(solution)/shard_map/pallas_call | solution.py:692

commit v5 on v4

--- a/solution.py
+++ b/solution.py
@@ -15,7 +15,8 @@
 W = 512
 HD = 128
 T = 8
-HALF = LEN // 2
+LOW = 32
+REST = LEN - LOW
 MESH = pl.DeviceIdType.MESH
 LIMIT = 64_600_000
 LAST = SEQS - 1
@@ -90,6 +91,8 @@
     m_rs,
     e_ss,
     e_rs,
+    fv_ss,
+    fv_rs,
     xs,
 ):
     phases = nsec.bit_length() - 1
@@ -124,7 +127,7 @@
         pltpu.make_async_copy(aw_h.at[0], aw_v, lsem.at[9]),
         pltpu.make_async_copy(wv_h, wv_v, lsem.at[10]),
         pltpu.make_async_copy(coef_h.at[0], coef_v, lsem.at[11]),
-        pltpu.make_async_copy(fvo_h.at[0], fvof.at[t, pl.ds(E, E)], lsem.at[12]),
+        pltpu.make_async_copy(fvo_h.at[0], fvof.at[t, 0, pl.ds(E, E)], lsem.at[12]),
     ]
 
     fo_v[...] = jnp.zeros_like(fo_v)
@@ -240,10 +243,11 @@
     def dv(b):
         return Gather(dvf, None, dv_ss, dv_rs, b, b, 0, LEN, short_routes(0, LEN))
 
-    dy_hi = Gather(dyf, dy_h, dy_ss, dy_rs, LAST, LAST, HALF, HALF, ring_routes(HALF, HALF))
-    dy_lo = Gather(dyf, dy_h, dy_ss, dy_rs, SEQS, LAST, 0, HALF, short_routes(0, HALF))
-    dv_hi = Gather(dvf, None, dv_ss, dv_rs, LAST, LAST, HALF, HALF, short_routes(HALF, HALF))
-    dv_lo = Gather(dvf, None, dv_ss, dv_rs, SEQS, LAST, 0, HALF, short_routes(0, HALF))
+    dy_hi = Gather(dyf, dy_h, dy_ss, dy_rs, LAST, LAST, LOW, REST, ring_routes(LOW, REST))
+    dy_lo = Gather(dyf, dy_h, dy_ss, dy_rs, SEQS, LAST, 0, LOW, short_routes(0, LOW))
+    dv_hi = Gather(dvf, None, dv_ss, dv_rs, LAST, LAST, LOW, REST, short_routes(LOW, REST))
+    dv_lo = Gather(dvf, None, dv_ss, dv_rs, SEQS, LAST, 0, LOW, short_routes(0, LOW))
+    fv = Gather(fvof, None, fv_ss, fv_rs, 0, 0, E, E, short_routes(E, E))
     own_kinds = (0, 1, 2, 3, 6)
     short_kinds = (2, 0, 1, 3)
 
@@ -297,9 +301,9 @@
         xf = x_v[b].astype(F32)
         scaled = (xf * g_v[...]).astype(BF16)
         sqt[t, b] = jnp.sum(lanes_folded(xf * xf).T, axis=0, keepdims=True)
-        part = contract(ao_v[b], fo_v[...])
-        part += contract(dyf[t, b], fs_v[...])
-        part += contract(scaled, fp_v[...])
+        part = contract(fo_v[...], ao_v[b])
+        part += contract(fs_v[...], dyf[t, b])
+        part += contract(fp_v[...], scaled)
         p_part[lax.rem(b, 2), b // 2] = part
         return carry
 
@@ -324,8 +328,8 @@
         dvf[t, b] = d_val.astype(BF16)
         dv(b).send(*short_kinds)
 
-    def half_terms(first, probs):
-        rows = pl.ds(first, HALF)
+    def part_terms(first, count, probs):
+        rows = pl.ds(first, count)
         acc = contract(dyf[0, LAST, rows], wo_v[:, 0:W])
         for k in range(1, T):
             acc += contract(dyf[k, LAST, rows], wo_v[:, k * W : (k + 1) * W])
@@ -401,6 +405,7 @@
         def _():
             for at in (8, 9, 10, 11, 12):
                 loads[at].wait()
+            fv.send(*short_kinds)
             ps_copy().wait_recv()
             for k in range(3):
                 p_snd[k] = p_part[core, k] + p_sib[k]
@@ -434,8 +439,8 @@
                 return carry
 
             lax.fori_loop(0, SEQS, turn, 0)
-            aw_hi[...] = aw_v[LAST, :, HALF:LEN].reshape(4 * HALF, LEN).T
-            aw_lo[...] = aw_v[LAST, :, 0:HALF].reshape(4 * HALF, LEN).T
+            aw_hi[...] = aw_v[LAST, :, LOW:LEN].reshape(4 * REST, LEN).T
+            aw_lo[...] = aw_v[LAST, :, 0:LOW].reshape(4 * LOW, LEN).T
 
         @pl.when(i >= 2)
         def _():
@@ -467,7 +472,7 @@
     dy_lo.arrived(1)
     dy_lo.send(6)
     relay(LAST - 3, LAST - 3, 0, LEN)
-    to_peers(fvo_h.at[0], fvof.at[t, pl.ds(E, E)], xs.at[6], xs.at[7])
+    share_vals(fv)
     for k in range(3):
 
         @pl.when(chip != k)
@@ -478,31 +483,17 @@
             ).start()
 
     dy_hi.arrived(3, 4)
-    terms = half_terms(HALF, aw_hi[...])
-    rest_v[...] = terms[0:HALF]
-    dvf[t, LAST, pl.ds(HALF, HALF)] = terms[HALF:LEN].astype(BF16)
+    terms = part_terms(LOW, REST, aw_hi[...])
+    rest_v[...] = terms[0:LOW]
+    dvf[t, LAST, pl.ds(LOW, REST)] = terms[LOW:LEN].astype(BF16)
     dv_hi.send(*short_kinds)
     dv(LAST - 2).arrived(3, 4)
     input_grad(LAST - 2, LAST - 2, 0, LEN)
 
     dy_lo.arrived(3, 4)
-    terms = half_terms(0, aw_lo[0:HALF])
-    dvf[t, LAST, pl.ds(0, HALF)] = (terms + rest_v[...]).astype(BF16)
+    terms = part_terms(0, LOW, aw_lo[0:LOW])
+    dvf[t, LAST, pl.ds(0, LOW)] = (terms + rest_v[...]).astype(BF16)
     dv_lo.send(*short_kinds)
-
-    share_vals(dv(LAST - 1))
-    share_vals(dv_hi)
-    relay(LAST - 2, LAST - 2, 0, LEN)
-    dv(LAST - 1).arrived(3, 4)
-    input_grad(LAST - 1, LAST - 1, 0, LEN)
-    share_vals(dv_lo)
-    dv_hi.arrived(3, 4)
-    input_grad(LAST, LAST, HALF, HALF)
-    dv_lo.arrived(3, 4)
-    input_grad(SEQS, LAST, 0, HALF)
-    relay(LAST - 1, LAST - 1, 0, LEN)
-    relay(LAST, LAST, HALF, HALF)
-    relay(SEQS, LAST, 0, HALF)
 
     fold_eig(phases - 1)
     damp = ev[0] * (0.1 / (nsec * 2 * E * E))
@@ -518,7 +509,21 @@
     col = lax.broadcasted_iota(jnp.int32, (E, W), 1)
     wk[E : 2 * E, W : 2 * W] = (lax.rem(col, E) == row).astype(F32)
 
-    both(fvof.at[pl.ds(0, T - 1), pl.ds(E, E)], xs.at[6], xs.at[7]).wait_recv()
+    share_vals(dv(LAST - 1))
+    share_vals(dv_hi)
+    relay(LAST - 2, LAST - 2, 0, LEN)
+    dv(LAST - 1).arrived(3, 4)
+    input_grad(LAST - 1, LAST - 1, 0, LEN)
+    share_vals(dv_lo)
+    dv_hi.arrived(3, 4)
+    input_grad(LAST, LAST, LOW, REST)
+    dv_lo.arrived(3, 4)
+    input_grad(SEQS, LAST, 0, LOW)
+    relay(LAST - 1, LAST - 1, 0, LEN)
+    relay(LAST, LAST, LOW, REST)
+    relay(SEQS, LAST, 0, LOW)
+
+    fv.arrived(3, 4)
     here = sc_h.at[:, pl.ds(pl.multiple_of(t * LEN, LEN), LEN)]
     keep = pltpu.make_async_copy(sc_v, here, lsem.at[14])
 
@@ -526,16 +531,23 @@
     def _():
         both(p_rcv.at[pl.ds(0, 3)], xs.at[8], xs.at[9]).wait_recv()
         proj = p_snd[chip] + p_rcv[0] + p_rcv[1] + p_rcv[2]
-        s_val = contract(dvf[0, t], fvof[0])
+        s_val = contract(dvf[0, t], fvof[0, 0])
         for k in range(1, T):
-            s_val += contract(dvf[k, t], fvof[k])
+            s_val += contract(dvf[k, t], fvof[k, 0])
         pick = wk[:, W : 2 * W]
 
         def exact(left, right):
             return jnp.dot(left, right, precision=HIGH, preferred_element_type=F32)
 
-        pairs = exact(proj, wk[:, 0:W]) * exact(proj, pick)
-        pairs += exact(proj * rb[t], wk[:, 2 * W : 3 * W]) * exact(s_val, pick)
+        def exact_turned(left, right):
+            return lax.dot_general(
+                left, right, (((0,), (0,)), ((), ())), precision=HIGH, preferred_element_type=F32
+            )
+
+        rows = slice(0, 3 * E)
+        pairs = exact_turned(proj, wk[rows, 0:W]) * exact_turned(proj, wk[rows, W : 2 * W])
+        proj = proj * rb[t].T[rows]
+        pairs += exact_turned(proj, wk[rows, 2 * W : 3 * W]) * exact(s_val, pick)
         row = lax.broadcasted_iota(jnp.int32, (Q, W), 0)
         col = lax.broadcasted_iota(jnp.int32, (Q, W), 1)
         group = (row == col // E).astype(F32)
@@ -559,7 +571,7 @@
     for gather in (dy_hi, dy_lo, dv_hi, dv_lo):
         gather.sent()
     both(sqt.at[pl.ds(0, T - 1)], xs.at[4], xs.at[5]).wait_send()
-    both(fvof.at[pl.ds(0, T - 1), pl.ds(E, E)], xs.at[6], xs.at[7]).wait_send()
+    fv.sent()
     ps_copy().wait_send()
 
     @pl.when(chip == 3)
@@ -633,19 +645,19 @@
             vmem((SEQS, 4, LEN, LEN), BF16),
             vmem((W, 2 * W), BF16),
             vmem((W, D), BF16),
-            vmem((128, W), BF16),
-            vmem((128, W), BF16),
-            vmem((128, W), BF16),
-            vmem((T, 128, HD), BF16),
+            vmem((3 * E, W), BF16),
+            vmem((3 * E, W), BF16),
+            vmem((3 * E, W), BF16),
+            vmem((T, 1, 128, HD), BF16),
             vmem((1, W), F32),
             vmem((2, Q, E, E), F32),
             vmem((2, E, E), F32),
             vmem(blocks, F32),
             vmem(blocks, BF16),
-            vmem((2, 3, LEN, 128), F32),
-            vmem((3, LEN, 128), F32),
-            vmem((3, LEN, 128), F32),
-            vmem((3, LEN, 128), F32),
+            vmem((2, 3, 3 * E, LEN), F32),
+            vmem((3, 3 * E, LEN), F32),
+            vmem((3, 3 * E, LEN), F32),
+            vmem((3, 3 * E, LEN), F32),
             vmem((T, SEQS, 1, 128), F32),
             vmem((SEQS, LEN, 128), F32),
             vmem((SLOTS, T, 1, 128), F32),
@@ -653,9 +665,9 @@
             vmem((128, 3 * W), F32),
             vmem((Q, LEN), F32),
             vmem(blocks, BF16),
-            vmem((LEN, 4 * HALF), BF16),
-            vmem((LEN, 4 * HALF), BF16),
-            vmem((HALF, HD), F32),
+            vmem((LEN, 4 * REST), BF16),
+            vmem((LEN, 4 * LOW), BF16),
+            vmem((LOW, HD), F32),
             pltpu.SemaphoreType.REGULAR((phases,)),
             dma((15,)),
             dma((SLOTS,)),
@@ -666,6 +678,8 @@
             dma((SLOTS,)),
             dma((phases,)),
             dma((phases,)),
+            dma((1,)),
+            dma((4, 1)),
             dma((12,)),
         ],
         compiler_params=pltpu.CompilerParams(

time: 65.6 us -> 64.6 us (0.985)
  Pallas kernels: 64.8 us -> 63.8 us
    pallas_call x1, Pallas kernels: 62.8 us -> 61.8 us  [per_device(): pl.pallas_call(functools.partial(kernel, nsec), out_shape=(jax.ShapeDtype...]
where the time goes in v5:
time: 64.6 us; the launch traced here: 64.5 us
  Pallas kernels  63.8 us (99%)
    pallas_call x1, Pallas kernels, per_device(): pl.pallas_call(functools.partial(kernel, nsec), out_shape=(jax.ShapeDtype...  61.8 us
    pallas_call x1, Pallas kernels, per_device(): pl.pallas_call(hand_over, out_shape=(jax.ShapeDtypeStruct(blocks, BF16),...  1.99 us

profile of v5, /device:TPU:102, one launch (start us, length us, event | category | flops | bytes accessed | tf_op | source)
XLA Modules:
  0.0 64.5 jit_solution(7596755434234328713)
XLA Ops:
  0.6 61.8 %shard_map.140 = (bf16[6,128,512]{2,1,0:T(8,128)(2,1)}, f32[16,768]{1,0:T(8,128)}) custom-call(bf16[6,128,512]{2,1,0:T(8,128)(2,1)} %bitcast.5, bf16[6,128,512]{2,1,0:T(8,128)(2,1)} %bitcast.6, f32[1,512]{1,0:T(1,128)} %g_h.1, bf16[1,6,4,128,128]{4,3,2,1,0:T(8,128)(2,1)} %aw_h.1, bf16[6,128,512]{2,1,0:T(8,128)(2,1)} %bitcast.7, bf16[512,1024]{1,0:T(8,128)(2,1)} %wv_h.1, ...), custom_call_target="tpu_custom_call" | custom-call | flops 8000000000 | bytes 10485760 | tf_op jit(solution)/shard_map/pallas_call | solution.py:632
  62.5 2.0 %shard_map.141 = (bf16[6,128,512]{2,1,0:T(8,128)(2,1)}, f32[16,768]{1,0:T(8,128)}) custom-call(bf16[6,128,512]{2,1,0:T(8,128)(2,1)} %get-tuple-element.6.gn_h, f32[16,768]{1,0:T(8,128)} %get-tuple-element.7.sc_h), custom_call_target="tpu_custom_call" | custom-call | tf_op jit(solution)/shard_map/pallas_call | solution.py:706
